TPU v7x, 128 devices: a whole 4x4x4 slice. The times are simulated.
128 devices in a mesh: chan: 32 (over x, z, y_hi), win: 4 (over y_lo, core).
Axes of the slice: x: 4, y: 4 (y_hi: 2, y_lo: 2; y = y_hi * 2 + y_lo), z: 4, core: 2. Of those that a mesh axis runs over, the one named last changes fastest.
Arguments:
- spectra: bfloat16 [2, 1024, 32, 768], P(None, 'chan', 'win'), may hold values from -6 to 6
- window_flags: int32 [32], P('win'), may hold values 0 or 1
- source_block: int32 [4], replicated, may hold values from 0 to 31
- offset_limit: int32 [4], replicated, may hold values from 32 to 1023
Outputs:
- correlations: bfloat16 [4, 32, 1024, 1536], P(None, 'win', 'chan')
All inputs are finite; a program needn't handle non-finite values. No bound on the sum of `window_flags` on one device may be relied on, other than what follows from the above.
Results may differ from a plain program's by a relative error of at most 0.0055.
Values may be sent and summed in bfloat16 or wider, within the bound.
A program may use at most 192 MiB of HBM per device.

v0:
```python
import math

import jax
import jax.numpy as jnp
from jax import lax
from jax.sharding import PartitionSpec as P

ROUNDS = 4


def from_root(block, axis, holder):
    block = jnp.where(lax.axis_index(axis) == holder, block, jnp.zeros_like(block))
    return lax.psum(block, axis)


def whiten(spectra):
    real = spectra[0].astype(jnp.float32)
    imag = spectra[1].astype(jnp.float32)
    power = real * real + imag * imag
    level = jnp.mean(power, axis=-1, keepdims=True)
    factor = lax.rsqrt(power + 0.25 * level + 1e-06)
    return jnp.stack([real * factor, imag * factor]).astype(jnp.bfloat16)


def lag_table(bins, windows):
    freq = jnp.arange(bins, dtype=jnp.int32)
    shifts = jnp.arange(2 * bins, dtype=jnp.int32) - bins
    phase = jnp.mod(freq[:, None] * shifts[None, :], 2 * bins).astype(jnp.float32)
    theta = phase * (math.pi / bins)
    weight = jnp.where(freq == 0, 1.0, 2.0).astype(jnp.float32) / math.sqrt(bins * windows)
    return jnp.concatenate(
        [weight[:, None] * jnp.cos(theta), -weight[:, None] * jnp.sin(theta)], axis=0
    )


def cross_stack(source, flagged):
    real = jnp.einsum("swf,cwf->scf", source[0], flagged[0], preferred_element_type=jnp.float32)
    real = real + jnp.einsum(
        "swf,cwf->scf", source[1], flagged[1], preferred_element_type=jnp.float32
    )
    imag = jnp.einsum("swf,cwf->scf", source[0], flagged[1], preferred_element_type=jnp.float32)
    imag = imag - jnp.einsum(
        "swf,cwf->scf", source[1], flagged[0], preferred_element_type=jnp.float32
    )
    return (real, imag)


def masked(real, imag, senders, receivers, limit):
    gap = jnp.abs(receivers[None, :] - senders[:, None])
    keep = ((gap >= 1) & (gap <= limit)).astype(jnp.float32)[..., None]
    return jnp.concatenate([real * keep, imag * keep], axis=-1)


def shards(spectra, window_flags, source_block, offset_limit):
    white = whiten(spectra)
    block = white.shape[1]
    bins = white.shape[3]
    groups = lax.axis_size("win")
    share = block // groups
    member = lax.axis_index("win")
    windows = window_flags.shape[0] * groups
    table = lag_table(bins, windows)
    receivers = lax.axis_index("chan") * block + jnp.arange(block, dtype=jnp.int32)
    flag_values = window_flags.astype(jnp.bfloat16)
    results = []
    every, every_flags = (
        lax.all_gather(white, "win", axis=2, tiled=True),
        lax.all_gather(flag_values, "win", axis=0, tiled=True),
    )
    flagged = every * every_flags[None, None, :, None]
    piece = lax.dynamic_slice_in_dim(every, member * share, share, 1)
    for step in range(ROUNDS):
        root = source_block[step]
        source = from_root(piece, "chan", root)
        real, imag = cross_stack(source, flagged)
        senders = root * block + member * share + jnp.arange(share, dtype=jnp.int32)
        stack = masked(real, imag, senders, receivers, offset_limit[step])
        corr = jnp.einsum("scf,fl->scl", stack, table, precision=lax.Precision.HIGHEST)
        results.append(corr.astype(jnp.bfloat16))
    return jnp.stack(results)


def solution(mesh):
    in_specs = (P(None, "chan", "win", None), P("win"), P(), P())
    out_specs = P(None, "win", "chan", None)
    return jax.shard_map(shards, mesh=mesh, in_specs=in_specs, out_specs=out_specs, check_vma=False)
```

profile of v0, /device:TPU:0, one launch (start us, length us, event | category | flops | bytes accessed | tf_op | source)
XLA Modules:
  0.0 631.6 jit_solution(818940323499873210)
XLA Ops:
  6.5 1.4 fusion.32
  7.9 1.4 fusion.30
  9.3 0.9 pad_maximum_fusion.1
  10.4 0.7 fusion.55
  13.6 36.8 %all-gather.2.cloned.1.call-done = bf16[2,32,32,768]{3,2,1,0:T(8,128)(2,1)} async-done(((bf16[2,32,8,768]{3,2,1,0:T(8,128)(2,1)}), bf16[2,32,32,768]{3,2,1,0:T(8,128)(2,1)}) %all-gather.2.cloned.1.call-update) | async-done | bytes 3145744 | tf_op jit(solution)/shard_map/all_gather | solution.py:67
  50.4 2.8 broadcast_select_fusion.3
  55.8 0.6 dynamic-slice
  57.3 6.2 all-reduce
  63.6 0.7 fusion.54
  64.2 2.6 fusion.42
  66.8 20.5 %cosine_multiply_fusion = (f32[768,1536]{1,0:T(8,128)}, f32[768,1536]{1,0:T(8,128)}) fusion(s32[1536]{0:T(1024)S(1)} %iota_add_fusion, f32[768]{0:T(1024)S(1)} %get-tuple-element.47, f32[768]{0:T(1024)S(1)} %get-tuple-element.48), kind=kLoop, calls=%fused_computation.5 | loop fusion | flops 12976128 | bytes 9449472 | tf_op jit(solution)/shard_map/mul | solution.py:32
  87.4 0.3 broadcast_multiply_fusion
  87.9 9.2 %copy.5 = bf16[32,32,768]{1,0,2:T(8,128)(2,1)} copy(bf16[32,32,768]{2,1,0:T(8,128)(2,1)S(1)} %get-tuple-element.9) | data formatting | bytes 3145728 | tf_op jit(solution)/shard_map/squeeze | solution.py:37
  97.0 9.2 %copy.8 = bf16[32,32,768]{1,0,2:T(8,128)(2,1)} copy(bf16[32,32,768]{2,1,0:T(8,128)(2,1)S(1)} %get-tuple-element.10) | data formatting | bytes 3145728 | tf_op jit(solution)/shard_map/squeeze | solution.py:39
  106.3 310.0 %all-reduce.4.cloned.1.call-done = (bf16[2,8,32,768]{3,2,1,0:T(8,128)(2,1)}, bf16[2,8,32,768]{3,2,1,0:T(8,128)(2,1)}, bf16[2,8,32,768]{3,2,1,0:T(8,128)(2,1)}, bf16[2,8,32,768]{3,2,1,0:T(8,128)(2,1)}) async-done(((bf16[2,8,32,768]{3,2,1,0:T(8,128)(2,1)}, bf16[2,8,32,768]{3,2,1,0:T(8,128)(2,1)}, bf16[2,8,32,768]{3,2,1,0:T(8,128)(2,1)}, bf16[2,8,32,768]{3,2,1,0:T(8,128)(2,1)}), ...) | async-done | bytes 3145744 | tf_op jit(solution)/shard_map/psum | solution.py:13
  416.3 1.5 slice_bitcast_fusion.2
  417.7 1.8 copy.27
  419.6 2.0 copy.25
  421.6 8.4 %fusion.71 = f32[768,32,8]{1,2,0:T(8,128)} fusion(bf16[32,32,768]{1,0,2:T(8,128)(2,1)} %copy.5, bf16[8,32,768]{1,0,2:T(8,128)(2,1)} %copy.27), kind=kOutput, calls=%fused_computation.119 | convolution fusion | flops 12582912 | bytes 2752512 | tf_op jit(solution)/shard_map/swf,cwf->scf/dot_general | solution.py:42
  430.0 5.0 fusion.68
  435.0 5.0 fusion.70
  440.1 5.1 fusion.69
  445.2 1.8 copy.19
  447.0 8.4 %fusion.64 = f32[768,32,8]{1,2,0:T(8,128)} fusion(bf16[32,32,768]{1,0,2:T(8,128)(2,1)} %copy.5, bf16[8,32,768]{1,0,2:T(8,128)(2,1)} %copy.19), kind=kOutput, calls=%fused_computation.112 | convolution fusion | flops 12582912 | bytes 2752512 | tf_op jit(solution)/shard_map/swf,cwf->scf/dot_general | solution.py:37
  455.4 5.0 fusion.66
  460.4 2.0 copy.21
  462.4 8.4 %fusion.67 = f32[768,32,8]{1,2,0:T(8,128)} fusion(bf16[32,32,768]{1,0,2:T(8,128)(2,1)} %copy.5, bf16[8,32,768]{1,0,2:T(8,128)(2,1)} %copy.21), kind=kOutput, calls=%fused_computation.115 | convolution fusion | flops 12582912 | bytes 2752512 | tf_op jit(solution)/shard_map/swf,cwf->scf/dot_general | solution.py:42
  470.9 5.0 fusion.65
  475.9 0.9 slice_bitcast_fusion.6
  476.8 2.9 copy.13
  479.6 8.4 %fusion.60 = f32[768,32,8]{1,2,0:T(8,128)} fusion(bf16[32,32,768]{1,0,2:T(8,128)(2,1)} %copy.5, bf16[8,32,768]{1,0,2:T(8,128)(2,1)} %copy.13), kind=kOutput, calls=%fused_computation.108 | convolution fusion | flops 12582912 | bytes 2752512 | tf_op jit(solution)/shard_map/swf,cwf->scf/dot_general | solution.py:37
  488.0 5.0 fusion.62
  493.0 1.9 copy.15
  494.9 8.4 %fusion.63 = f32[768,32,8]{1,2,0:T(8,128)} fusion(bf16[32,32,768]{1,0,2:T(8,128)(2,1)} %copy.5, bf16[8,32,768]{1,0,2:T(8,128)(2,1)} %copy.15), kind=kOutput, calls=%fused_computation.111 | convolution fusion | flops 12582912 | bytes 2752512 | tf_op jit(solution)/shard_map/swf,cwf->scf/dot_general | solution.py:42
  503.4 5.0 fusion.61
  508.4 2.2 copy.6
  510.6 8.5 %fusion.56 = f32[768,32,8]{1,2,0:T(8,128)} fusion(bf16[32,32,768]{1,0,2:T(8,128)(2,1)} %copy.5, bf16[8,32,768]{1,0,2:T(8,128)(2,1)} %copy.6), kind=kOutput, calls=%fused_computation.104 | convolution fusion | flops 12582912 | bytes 2752512 | tf_op jit(solution)/shard_map/swf,cwf->scf/dot_general | solution.py:37
  519.1 5.0 fusion.58
  524.2 1.9 copy.9
  526.1 8.4 %fusion.59 = f32[768,32,8]{1,2,0:T(8,128)} fusion(bf16[32,32,768]{1,0,2:T(8,128)(2,1)} %copy.5, bf16[8,32,768]{1,0,2:T(8,128)(2,1)} %copy.9), kind=kOutput, calls=%fused_computation.107 | convolution fusion | flops 12582912 | bytes 2752512 | tf_op jit(solution)/shard_map/swf,cwf->scf/dot_general | solution.py:42
  534.4 5.0 fusion.57
  539.4 3.3 copy.30
  542.7 1.9 copy.26
  544.6 3.3 copy.24
  547.8 1.9 copy.20
  549.7 3.3 copy.18
  553.0 1.9 copy.14
  554.9 3.3 copy.7
  558.1 3.1 copy.12
  561.2 2.0 copy.29
  563.3 3.3 copy.28
  566.6 1.9 copy.23
  568.5 3.3 copy.22
  571.7 1.9 copy.17
  573.6 3.2 copy.16
  576.9 3.2 copy.10
  580.0 2.0 copy.11
  582.0 2.2 bitcast_multiply_fusion.5
  584.3 12.3 %fusion.15 = bf16[1,8,32,1536]{3,2,1,0:T(8,128)(2,1)S(1)} fusion(f32[768,1536]{1,0:T(8,128)} %get-tuple-element.26, f32[768,1536]{1,0:T(8,128)} %get-tuple-element.25, f32[8,32,768]{2,1,0:T(8,128)S(1)} %get-tuple-element.30, f32[8,32,768]{2,1,0:T(8,128)S(1)} %get-tuple-element.29), kind=kOutput, calls=%fused_computation.21 | convolution fusion | flops 7250903040 | bytes 11796480 | tf_op jit(solution)/shard_map/scf,fl->scl/dot_general | solution.py:78
  597.0 8.2 %fusion.14 = bf16[1,8,32,1536]{3,2,1,0:T(8,128)(2,1)S(1)} fusion(f32[768,1536]{1,0:T(8,128)S(1)} %bitcast.126, f32[768,1536]{1,0:T(8,128)S(1)} %bitcast.124, f32[8,32,768]{2,1,0:T(8,128)S(1)} %get-tuple-element.32, f32[8,32,768]{2,1,0:T(8,128)S(1)} %get-tuple-element.31), kind=kOutput, calls=%fused_computation.20 | convolution fusion | flops 7250903040 | bytes 11796480 | tf_op jit(solution)/shard_map/scf,fl->scl/dot_general | solution.py:78
  605.2 0.3 bitcast_multiply_fusion.1
  605.5 8.4 %fusion.13 = bf16[1,8,32,1536]{3,2,1,0:T(8,128)(2,1)S(1)} fusion(f32[768,1536]{1,0:T(8,128)S(1)} %bitcast.126, f32[768,1536]{1,0:T(8,128)S(1)} %bitcast.124, f32[8,32,768]{2,1,0:T(8,128)S(1)} %get-tuple-element.34, f32[8,32,768]{2,1,0:T(8,128)S(1)} %get-tuple-element.33), kind=kOutput, calls=%fused_computation.19 | convolution fusion | flops 7250903040 | bytes 11796480 | tf_op jit(solution)/shard_map/scf,fl->scl/dot_general | solution.py:78
  614.3 8.2 %fusion.16 = bf16[1,8,32,1536]{3,2,1,0:T(8,128)(2,1)S(1)} fusion(f32[768,1536]{1,0:T(8,128)S(1)} %bitcast.126, f32[768,1536]{1,0:T(8,128)S(1)} %bitcast.124, f32[8,32,768]{2,1,0:T(8,128)S(1)} %get-tuple-element.28, f32[8,32,768]{2,1,0:T(8,128)S(1)} %get-tuple-element.27), kind=kOutput, calls=%fused_computation.22 | convolution fusion | flops 7250903040 | bytes 11796480 | tf_op jit(solution)/shard_map/scf,fl->scl/dot_general | solution.py:78
  622.4 1.9 pad_maximum_fusion
  (134 shorter events, 1.3 us)
Async XLA Ops:
  6.5 3.8 copy-start.30
  6.5 43.8 %all-gather.2.cloned.1.call-start = ((), (), s32[]{:S(2)}) async-start(), calls=%async_computation | async-start | bytes 3932160 | tf_op jit(solution)/shard_map/all_gather | solution.py:67
  10.3 406.0 %all-reduce.4.cloned.1.call-start = ((), (), s32[]{:S(2)}) async-start(), calls=%async_computation.1 | async-start | bytes 6291456 | tf_op jit(solution)/shard_map/psum | solution.py:13
  13.5 42.2 %copy-start.32 = (s32[8]{0:T(128)S(1)}, s32[8]{0:T(128)}, u32[]{:S(2)}) copy-start(s32[8]{0:T(128)} %param.5) | copy-start | bytes 100
  13.5 42.2 %copy-start.33 = (u32[128]{0:T(128)S(1)}, u32[128]{0:T(128)}, u32[]{:S(2)}) copy-start(u32[128]{0:T(128)} %constant.54) | copy-start | bytes 1540
  13.6 50.0 %copy-start.31 = (s32[4]{0:T(128)S(1)}, s32[4]{0:T(128)}, u32[]{:S(2)}) copy-start(s32[4]{0:T(128)} %param.7) | copy-start | bytes 52
  66.8 20.5 %copy-start.15 = (bf16[2,32,32,768]{3,2,1,0:T(8,128)(2,1)S(1)}, bf16[2,32,32,768]{3,2,1,0:T(8,128)(2,1)}, u32[]{:S(2)}) copy-start(bf16[2,32,32,768]{3,2,1,0:T(8,128)(2,1)} %all-gather.2.cloned.1.call-done) | copy-start | bytes 9437188
  419.6 10.4 %slice-start = ((s8[6291456]{0:T(1024)(128)(4,1)}), s8[2097152]{0:T(1024)(128)(4,1)S(1)}, s32[]{:S(2)}) async-start(s8[6291456]{0:T(1024)(128)(4,1)} %bitcast.107), calls=%async_computation.2 | async-start | bytes 4194304
  421.6 8.4 %slice-start.1 = ((s8[6291456]{0:T(1024)(128)(4,1)}), s8[4194304]{0:T(1024)(128)(4,1)S(1)}, s32[]{:S(2)}) async-start(s8[6291456]{0:T(1024)(128)(4,1)} %bitcast.107), calls=%async_computation.3 | async-start | bytes 8388608
  421.6 8.4 %copy-start.2 = (bf16[8,32,768]{1,0,2:T(8,128)(2,1)S(1)}, bf16[8,32,768]{1,0,2:T(8,128)(2,1)}, u32[]{:S(2)}) copy-start(bf16[8,32,768]{1,0,2:T(8,128)(2,1)} %copy.25) | copy-start | bytes 1179652
  421.6 13.4 %slice-start.2 = ((s8[6291456]{0:T(1024)(128)(4,1)}), s8[4194304]{0:T(1024)(128)(4,1)S(1)}, s32[]{:S(2)}) async-start(s8[6291456]{0:T(1024)(128)(4,1)} %bitcast.109), calls=%async_computation.4 | async-start | bytes 8388608
  430.0 5.0 slice-start.3
  435.0 5.0 copy-start
  445.1 10.2 %slice-start.4 = ((s8[6291456]{0:T(1024)(128)(4,1)}), s8[2097152]{0:T(1024)(128)(4,1)S(1)}, s32[]{:S(2)}) async-start(s8[6291456]{0:T(1024)(128)(4,1)} %bitcast.111), calls=%async_computation.6 | async-start | bytes 4194304
  447.0 8.4 %slice-start.5 = ((s8[6291456]{0:T(1024)(128)(4,1)}), s8[4194304]{0:T(1024)(128)(4,1)S(1)}, s32[]{:S(2)}) async-start(s8[6291456]{0:T(1024)(128)(4,1)} %bitcast.111), calls=%async_computation.7 | async-start | bytes 8388608
  447.0 8.4 %copy-start.3 = (bf16[8,32,768]{1,0,2:T(8,128)(2,1)S(1)}, bf16[8,32,768]{1,0,2:T(8,128)(2,1)}, u32[]{:S(2)}) copy-start(bf16[8,32,768]{1,0,2:T(8,128)(2,1)} %copy.19) | copy-start | bytes 1179652
  460.4 10.5 %slice-start.6 = ((s8[6291456]{0:T(1024)(128)(4,1)}), s8[2097152]{0:T(1024)(128)(4,1)S(1)}, s32[]{:S(2)}) async-start(s8[6291456]{0:T(1024)(128)(4,1)} %bitcast.113), calls=%async_computation.8 | async-start | bytes 4194304
  462.4 8.5 %slice-start.7 = ((s8[6291456]{0:T(1024)(128)(4,1)}), s8[4194304]{0:T(1024)(128)(4,1)S(1)}, s32[]{:S(2)}) async-start(s8[6291456]{0:T(1024)(128)(4,1)} %bitcast.113), calls=%async_computation.9 | async-start | bytes 8388608
  462.4 8.5 %copy-start.4 = (bf16[8,32,768]{1,0,2:T(8,128)(2,1)S(1)}, bf16[8,32,768]{1,0,2:T(8,128)(2,1)}, u32[]{:S(2)}) copy-start(bf16[8,32,768]{1,0,2:T(8,128)(2,1)} %copy.21) | copy-start | bytes 1179652
  470.9 5.0 copy-start.28
  470.9 5.0 copy-start.29
  476.8 11.2 %slice-start.8 = ((s8[6291456]{0:T(1024)(128)(4,1)}), s8[2097152]{0:T(1024)(128)(4,1)S(1)}, s32[]{:S(2)}) async-start(s8[6291456]{0:T(1024)(128)(4,1)} %bitcast.115), calls=%async_computation.10 | async-start | bytes 4194304
  479.6 8.4 %slice-start.9 = ((s8[6291456]{0:T(1024)(128)(4,1)}), s8[4194304]{0:T(1024)(128)(4,1)S(1)}, s32[]{:S(2)}) async-start(s8[6291456]{0:T(1024)(128)(4,1)} %bitcast.115), calls=%async_computation.11 | async-start | bytes 8388608
  479.6 8.4 %copy-start.5 = (bf16[8,32,768]{1,0,2:T(8,128)(2,1)S(1)}, bf16[8,32,768]{1,0,2:T(8,128)(2,1)}, u32[]{:S(2)}) copy-start(bf16[8,32,768]{1,0,2:T(8,128)(2,1)} %copy.13) | copy-start | bytes 1179652
  493.0 10.3 %slice-start.10 = ((s8[6291456]{0:T(1024)(128)(4,1)}), s8[2097152]{0:T(1024)(128)(4,1)S(1)}, s32[]{:S(2)}) async-start(s8[6291456]{0:T(1024)(128)(4,1)} %bitcast.117), calls=%async_computation.12 | async-start | bytes 4194304
  494.9 8.4 %slice-start.11 = ((s8[6291456]{0:T(1024)(128)(4,1)}), s8[4194304]{0:T(1024)(128)(4,1)S(1)}, s32[]{:S(2)}) async-start(s8[6291456]{0:T(1024)(128)(4,1)} %bitcast.117), calls=%async_computation.13 | async-start | bytes 8388608
  494.9 8.4 %copy-start.6 = (bf16[8,32,768]{1,0,2:T(8,128)(2,1)S(1)}, bf16[8,32,768]{1,0,2:T(8,128)(2,1)}, u32[]{:S(2)}) copy-start(bf16[8,32,768]{1,0,2:T(8,128)(2,1)} %copy.15) | copy-start | bytes 1179652
  508.4 10.7 %slice-start.12 = ((s8[6291456]{0:T(1024)(128)(4,1)}), s8[2097152]{0:T(1024)(128)(4,1)S(1)}, s32[]{:S(2)}) async-start(s8[6291456]{0:T(1024)(128)(4,1)} %bitcast.119), calls=%async_computation.14 | async-start | bytes 4194304
  510.6 8.5 %slice-start.13 = ((s8[6291456]{0:T(1024)(128)(4,1)}), s8[4194304]{0:T(1024)(128)(4,1)S(1)}, s32[]{:S(2)}) async-start(s8[6291456]{0:T(1024)(128)(4,1)} %bitcast.119), calls=%async_computation.15 | async-start | bytes 8388608
  510.6 8.5 %copy-start.7 = (bf16[8,32,768]{1,0,2:T(8,128)(2,1)S(1)}, bf16[8,32,768]{1,0,2:T(8,128)(2,1)}, u32[]{:S(2)}) copy-start(bf16[8,32,768]{1,0,2:T(8,128)(2,1)} %copy.6) | copy-start | bytes 1179652
  524.2 10.2 %slice-start.14 = ((s8[6291456]{0:T(1024)(128)(4,1)}), s8[2097152]{0:T(1024)(128)(4,1)S(1)}, s32[]{:S(2)}) async-start(s8[6291456]{0:T(1024)(128)(4,1)} %bitcast.121), calls=%async_computation.16 | async-start | bytes 4194304
  526.1 8.4 %slice-start.15 = ((s8[6291456]{0:T(1024)(128)(4,1)}), s8[4194304]{0:T(1024)(128)(4,1)S(1)}, s32[]{:S(2)}) async-start(s8[6291456]{0:T(1024)(128)(4,1)} %bitcast.121), calls=%async_computation.17 | async-start | bytes 8388608
  526.1 8.4 %copy-start.1 = (bf16[8,32,768]{1,0,2:T(8,128)(2,1)S(1)}, bf16[8,32,768]{1,0,2:T(8,128)(2,1)}, u32[]{:S(2)}) copy-start(bf16[8,32,768]{1,0,2:T(8,128)(2,1)} %copy.9) | copy-start | bytes 1179652
  539.4 3.3 copy-start.10
  544.6 3.3 copy-start.11
  549.7 3.3 copy-start.14
  554.9 6.4 %copy-start.8 = (f32[768,32,8]{1,2,0:T(8,128)S(1)}, f32[768,32,8]{1,2,0:T(8,128)}, u32[]{:S(2)}) copy-start(f32[768,32,8]{1,2,0:T(8,128)} %fusion.70) | copy-start | bytes 2359300
  563.3 3.3 copy-start.9
  568.5 3.3 copy-start.12
  573.6 6.4 %copy-start.13 = (f32[768,32,8]{1,2,0:T(8,128)S(1)}, f32[768,32,8]{1,2,0:T(8,128)}, u32[]{:S(2)}) copy-start(f32[768,32,8]{1,2,0:T(8,128)} %fusion.58) | copy-start | bytes 2359300
  582.0 14.9 %slice-start.16 = ((s8[4718592]{0:T(1024)(128)(4,1)}), s8[4194304]{0:T(1024)(128)(4,1)S(1)}, s32[]{:S(2)}) async-start(s8[4718592]{0:T(1024)(128)(4,1)} %bitcast.123), calls=%async_computation.18 | async-start | bytes 8388608
  582.0 14.9 %slice-start.18 = ((s8[4718592]{0:T(1024)(128)(4,1)}), s8[4194304]{0:T(1024)(128)(4,1)S(1)}, s32[]{:S(2)}) async-start(s8[4718592]{0:T(1024)(128)(4,1)} %bitcast.125), calls=%async_computation.20 | async-start | bytes 8388608
  584.2 12.4 %copy-start.24 = (f32[768,32,8]{0,1,2:T(8,128)S(1)}, f32[768,32,8]{0,1,2:T(8,128)}, u32[]{:S(2)}) copy-start(f32[768,32,8]{0,1,2:T(8,128)} %copy.24) | copy-start | bytes 2359300
  584.2 12.4 %copy-start.25 = (f32[768,32,8]{0,1,2:T(8,128)S(1)}, f32[768,32,8]{0,1,2:T(8,128)}, u32[]{:S(2)}) copy-start(f32[768,32,8]{0,1,2:T(8,128)} %copy.20) | copy-start | bytes 2359300
  584.2 12.4 %copy-start.26 = (f32[768,32,8]{0,1,2:T(8,128)S(1)}, f32[768,32,8]{0,1,2:T(8,128)}, u32[]{:S(2)}) copy-start(f32[768,32,8]{0,1,2:T(8,128)} %copy.23) | copy-start | bytes 2359300
  584.3 12.4 %copy-start.27 = (f32[768,32,8]{0,1,2:T(8,128)S(1)}, f32[768,32,8]{0,1,2:T(8,128)}, u32[]{:S(2)}) copy-start(f32[768,32,8]{0,1,2:T(8,128)} %copy.22) | copy-start | bytes 2359300
  584.3 12.7 %slice-start.17 = ((s8[4718592]{0:T(1024)(128)(4,1)}), s8[524288]{0:T(1024)(128)(4,1)S(1)}, s32[]{:S(2)}) async-start(s8[4718592]{0:T(1024)(128)(4,1)} %bitcast.123), calls=%async_computation.19 | async-start | bytes 1048576
  584.3 12.7 %slice-start.19 = ((s8[4718592]{0:T(1024)(128)(4,1)}), s8[524288]{0:T(1024)(128)(4,1)S(1)}, s32[]{:S(2)}) async-start(s8[4718592]{0:T(1024)(128)(4,1)} %bitcast.125), calls=%async_computation.21 | async-start | bytes 1048576
  597.0 8.2 %copy-start.17 = (f32[768,32,8]{0,1,2:T(8,128)S(1)}, f32[768,32,8]{0,1,2:T(8,128)}, u32[]{:S(2)}) copy-start(f32[768,32,8]{0,1,2:T(8,128)} %copy.30) | copy-start | bytes 2359300
  597.0 8.2 %copy-start.19 = (f32[768,32,8]{0,1,2:T(8,128)S(1)}, f32[768,32,8]{0,1,2:T(8,128)}, u32[]{:S(2)}) copy-start(f32[768,32,8]{0,1,2:T(8,128)} %copy.26) | copy-start | bytes 2359300
  597.0 8.2 %copy-start.21 = (f32[768,32,8]{0,1,2:T(8,128)S(1)}, f32[768,32,8]{0,1,2:T(8,128)}, u32[]{:S(2)}) copy-start(f32[768,32,8]{0,1,2:T(8,128)} %copy.29) | copy-start | bytes 2359300
  597.0 8.2 %copy-start.23 = (f32[768,32,8]{0,1,2:T(8,128)S(1)}, f32[768,32,8]{0,1,2:T(8,128)}, u32[]{:S(2)}) copy-start(f32[768,32,8]{0,1,2:T(8,128)} %copy.28) | copy-start | bytes 2359300
  605.5 8.5 %copy-start.16 = (f32[768,32,8]{0,1,2:T(8,128)S(1)}, f32[768,32,8]{0,1,2:T(8,128)}, u32[]{:S(2)}) copy-start(f32[768,32,8]{0,1,2:T(8,128)} %copy.7) | copy-start | bytes 2359300
  605.5 8.5 %copy-start.18 = (f32[768,32,8]{0,1,2:T(8,128)S(1)}, f32[768,32,8]{0,1,2:T(8,128)}, u32[]{:S(2)}) copy-start(f32[768,32,8]{0,1,2:T(8,128)} %copy.12) | copy-start | bytes 2359300
  605.5 8.5 %copy-start.20 = (f32[768,32,8]{0,1,2:T(8,128)S(1)}, f32[768,32,8]{0,1,2:T(8,128)}, u32[]{:S(2)}) copy-start(f32[768,32,8]{0,1,2:T(8,128)} %copy.10) | copy-start | bytes 2359300
  605.5 8.5 %copy-start.22 = (f32[768,32,8]{0,1,2:T(8,128)S(1)}, f32[768,32,8]{0,1,2:T(8,128)}, u32[]{:S(2)}) copy-start(f32[768,32,8]{0,1,2:T(8,128)} %copy.11) | copy-start | bytes 2359300
Sparse Core Ops, SparseCore 0:
  10.4 39.9 all-gather.1
  53.4 362.8 all-reduce.3
where the time goes:
time: 637 us; the launch traced here: 632 us
  waiting for transfers between devices  347 us (54%)
  matrix products  141 us (22%)
  local copies, waits for them, and re-layouts  82.4 us (13%)
  other arithmetic  34.8 us (5%)
  between operations  20.2 us (3%)
    psum x1, waiting for transfers between devices, from_root(): return lax.psum(block, axis)  310 us
    dot_general x4, matrix products, shards(): jnp.einsum('scf,fl->scl', stack, table, precision=lax.Precision.HIGHEST)  37.1 us
    all_gather x1, waiting for transfers between devices, shards(): lax.all_gather(white, 'win', axis=2, tiled=True)  36.8 us
    dot_general x4, matrix products, cross_stack(): jnp.einsum('swf,cwf->scf', source[1], flagged[0], preferred_element_type=...  33.6 us
    dot_general x4, matrix products, cross_stack(): jnp.einsum('swf,cwf->scf', source[0], flagged[0], preferred_element_type=...  30.2 us
    mul x1, other arithmetic, lag_table(): weight[:, None] * jnp.cos(theta)  20.5 us
    dot_general x4, matrix products, cross_stack(): jnp.einsum('swf,cwf->scf', source[0], flagged[1], preferred_element_type=...  20.1 us
    dot_general x4, matrix products, cross_stack(): jnp.einsum('swf,cwf->scf', source[1], flagged[1], preferred_element_type=...  20.1 us
  transfers between devices with their start and end apart: 2, of which 2 were waited for; matrix products, arithmetic and copies ran while one was open for 7% of the time, Pallas kernels for 0%

commit v1 on v0

v1 whole, which is shorter than its diff:
```python
import math

import jax
import jax.numpy as jnp
import numpy as np
from jax import lax
from jax.experimental import pallas as pl
from jax.experimental.pallas import tpu as pltpu
from jax.sharding import PartitionSpec as P

MESH = pl.DeviceIdType.MESH
F = 768
HALF = 384
R = 4
SCALE = 1.0 / math.sqrt(24576.0)


def constants():
    rows = np.zeros((256, 256), np.float32)
    for wp in range(4):
        for p in range(4):
            for w2 in range(2):
                for c in range(8):
                    rows[((wp * 4 + p) * 2 + w2) * 8 + c, (p * 8 + c) * 8 + wp * 2 + w2] = 1.0
    cols = np.zeros((256, 256), np.float32)
    for i in range(128):
        cols[2 * i, i] = 1.0
        cols[2 * i + 1, 128 + i] = 1.0
    k = (256 * np.arange(3)[:, None] + 2 * np.arange(128)[None, :]).reshape(-1)
    lag = np.arange(768) - 768
    table = np.zeros((2, 768, 768), np.float32)
    for h in range(2):
        kk = k + h
        m = (kk[:, None] * lag[None, :]) % 1536
        g = np.where(kk == 0, 1.0, 2.0)[:, None]
        table[h, :HALF] = g * np.cos(np.pi * m / 768.0)
        table[h, HALF:] = -g * np.sin(np.pi * m / 768.0)
    return rows, cols, table


def coords():
    c, w = lax.axis_index("chan"), lax.axis_index("win")
    return c // 8, (c // 2) % 4, c % 2, w


def dev(x, z, yh, j):
    return (x * 8 + z * 2 + yh, j)


def whiten_into(spec_ref, flag_ref, rows_ref, cols_ref, out):
    for wp in range(4):
        part = []
        for reim in range(2):
            moved = jnp.dot(rows_ref[pl.ds(wp * 64, 64), :], spec_ref[reim], preferred_element_type=jnp.float32)
            moved = moved.astype(jnp.bfloat16)
            cut = [
                jnp.dot(moved[:, 256 * b:256 * b + 256], cols_ref[...], preferred_element_type=jnp.float32)
                for b in range(3)
            ]
            even = jnp.concatenate([c[:, :128] for c in cut], axis=1)
            odd = jnp.concatenate([c[:, 128:] for c in cut], axis=1)
            part.append((even, odd))
        (re0, re1), (im0, im1) = part
        p0 = re0 * re0 + im0 * im0
        p1 = re1 * re1 + im1 * im1
        level = (jnp.sum(p0, axis=1, keepdims=True) + jnp.sum(p1, axis=1, keepdims=True)) * (1.0 / F)
        base = 0.25 * level + 1e-06
        row = lax.broadcasted_iota(jnp.int32, (64, 1), 0)
        f0 = flag_ref[2 * wp].astype(jnp.float32)
        f1 = flag_ref[2 * wp + 1].astype(jnp.float32)
        flag = jnp.where((row // 8) % 2 == 0, f0, f1)
        q0 = lax.rsqrt(p0 + base) * flag
        q1 = lax.rsqrt(p1 + base) * flag
        for reim, h, v in ((0, 0, re0 * q0), (0, 1, re1 * q1), (1, 0, im0 * q0), (1, 1, im1 * q1)):
            out[reim * 8 + wp * 2 + h] = v.astype(jnp.bfloat16).reshape(4, 16, HALF)


def comm_kernel(block_ref, flag_ref, spec_ref, rows_ref, cols_ref, recv_out, src_out,
                recv, cand, pick, diag, src,
                a_s, a_r, d_s, d_r, p_s, p_r, g_s, g_r, f_s, f_r, o_s, t_s, t_r, u_s, u_r):
    x, z, yh, j = coords()
    slot = x * 4 + z
    bar = pltpu.get_barrier_semaphore()
    plane = []
    for t in range(1, 16):
        to = (slot + t) % 16
        plane.append((to, dev(to // 4, to % 4, yh, j)))
    column = []
    for t in range(1, 8):
        column.append((t, (j + t) % 4, dev(x, z, (yh + t // 4) % 2, (j + t) % 4)))
    for _, d in plane:
        pl.semaphore_signal(bar, inc=1, device_id=d, device_id_type=MESH)
    for _, _, d in column:
        pl.semaphore_signal(bar, inc=1, device_id=d, device_id_type=MESH)

    whiten_into(spec_ref, flag_ref, rows_ref, cols_ref, recv.at[j])
    pl.semaphore_wait(bar, 22)
    sends = []

    def send(s, d, ss, rs, to):
        c = pltpu.make_async_remote_copy(
            src_ref=s, dst_ref=d, send_sem=ss, recv_sem=rs, device_id=to, device_id_type=MESH)
        c.start()
        sends.append(c)
        return c

    mate = dev(x, z, yh, j + 1 - 2 * (j % 2))
    across = (j + 2) % 4
    other = dev(x, z, yh, across)
    swap = [send(recv.at[j, to], cand.at[slot], a_s.at[t], a_r.at[t], d) for t, (to, d) in enumerate(plane)]
    over = [
        send(recv.at[j, pl.ds(4 * q, 4)], recv.at[j, pl.ds(4 * q, 4)], g_s.at[q], g_r.at[q], other)
        for q in range(4)
    ]
    to_mate = send(recv.at[j], recv.at[j], p_s.at[0], p_r.at[0], mate)
    cand[slot] = recv[j, slot]

    relayed = []

    def relay(q):
        over[q].wait_recv()
        relayed.append(send(recv.at[across, pl.ds(4 * q, 4)], recv.at[across, pl.ds(4 * q, 4)], f_s.at[q], f_r.at[q], mate))

    for c in swap:
        c.wait_recv()
    for r in range(R):
        pick[:, r] = cand[block_ref[r] // 2]
    meet = [send(pick.at[p], diag.at[yh, j], d_s.at[t], d_r.at[t], d) for t, p, d in column]
    diag[yh, j] = pick[j]
    relay(0)
    for c in meet:
        c.wait_recv()
    for r in range(R):
        got = diag[block_ref[r] % 2, :, r]
        src[0, r, x, z] = got[0:2]
        src[1, r, x, z] = got[2:4]
    first = []
    for d in range(1, 4):
        z2, x2 = (z + d) % 4, (x + d) % 4
        first.append(send(src.at[0, :, x, z], src.at[0, :, x, z], t_s.at[0, d], t_r.at[0, d], dev(x, z2, yh, j)))
        first.append(send(src.at[1, :, x, z], src.at[1, :, x, z], t_s.at[1, d], t_r.at[1, d], dev(x2, z, yh, j)))
    relay(1)
    for c in first:
        c.wait_recv()
    second = []
    for r in range(R):
        for d in range(1, 4):
            z2, x2 = (z + d) % 4, (x + d) % 4
            second.append(send(src.at[0, r, x], src.at[0, r, x], u_s.at[0, r, d], u_r.at[0, r, d], dev(x2, z, yh, j)))
            second.append(send(src.at[1, r, :, z], src.at[1, r, :, z], u_s.at[1, r, d], u_r.at[1, r, d], dev(x, z2, yh, j)))
    relay(2)
    relay(3)
    to_mate.wait_recv()
    for c in relayed:
        c.wait_recv()
    out1 = pltpu.make_async_copy(recv, recv_out, o_s.at[0])
    out1.start()
    for c in second:
        c.wait_recv()
    out2 = pltpu.make_async_copy(src, src_out, o_s.at[1])
    out2.start()
    out1.wait()
    out2.wait()
    for c in sends:
        c.wait_send()


def comm(block, flags, spec, rows, cols):
    bf = jnp.bfloat16
    dma = pltpu.SemaphoreType.DMA
    vm = pl.BlockSpec(memory_space=pltpu.VMEM)
    sm = pl.BlockSpec(memory_space=pltpu.SMEM)
    return pl.pallas_call(
        comm_kernel,
        out_shape=(
            jax.ShapeDtypeStruct((4, 16, 4, 16, HALF), bf),
            jax.ShapeDtypeStruct((2, R, 4, 4, 2, 16, HALF), bf),
        ),
        in_specs=[sm, sm, vm, vm, vm],
        out_specs=[pl.BlockSpec(memory_space=pl.ANY)] * 2,
        scratch_shapes=[
            pltpu.VMEM((4, 16, 4, 16, HALF), bf),
            pltpu.VMEM((16, 4, 16, HALF), bf),
            pltpu.VMEM((4, R, 16, HALF), bf),
            pltpu.VMEM((2, 4, R, 16, HALF), bf),
            pltpu.VMEM((2, R, 4, 4, 2, 16, HALF), bf),
            dma((16,)), dma((16,)), dma((8,)), dma((8,)), dma((1,)), dma((1,)),
            dma((4,)), dma((4,)), dma((4,)), dma((4,)), dma((2,)),
            dma((2, 4)), dma((2, 4)), dma((2, R, 4)), dma((2, R, 4)),
        ],
        compiler_params=pltpu.CompilerParams(
            collective_id=1, has_side_effects=True, vmem_limit_bytes=50 * 2**20),
        name="comm",
    )(block, flags, spec, rows, cols)


def corr_kernel(block_ref, limit_ref, recv_ref, src_ref, table_ref, out_ref,
                xr, xi, yr, yi, yd, stack):
    chan, member = lax.axis_index("chan"), lax.axis_index("win")
    r = pl.program_id(0)

    @pl.when(r == 0)
    def _():
        @pl.loop(0, 16)
        def _(n):
            a, wp = n // 4, n % 4
            for h in range(2):
                for reim, to in ((0, xr), (1, xi)):
                    for p in range(4):
                        v = recv_ref[a, reim * 8 + wp * 2 + h, p].astype(jnp.float32)
                        for b in range(3):
                            for w2 in range(2):
                                to[h * 3 + b, n * 2 + w2, p] = v[8 * w2:8 * w2 + 8, 128 * b:128 * b + 128]

    @pl.loop(0, 16)
    def _(n):
        a, wp = n // 4, n % 4
        for h in range(2):
            lo, hi = wp * 2 + h, 8 + wp * 2 + h
            vr = src_ref[a // 2, 0, lo // 4, lo % 4, a % 2].astype(jnp.float32)
            vi = src_ref[a // 2, 0, hi // 4, hi % 4, a % 2].astype(jnp.float32)
            for b in range(3):
                for w2 in range(2):
                    cr = vr[8 * w2:8 * w2 + 8, 128 * b:128 * b + 128]
                    ci = vi[8 * w2:8 * w2 + 8, 128 * b:128 * b + 128]
                    yr[h * 3 + b, n * 2 + w2] = cr
                    yi[h * 3 + b, n * 2 + w2] = ci
                    yd[h * 3 + b, n * 2 + w2] = cr - ci

    root, limit = block_ref[r], limit_ref[r]
    c8 = lax.broadcasted_iota(jnp.int32, (8, 1), 0)
    SB = 2
    for h in range(2):
        @pl.loop(0, 3 * (8 // SB))
        def _(n):
            b, s0 = n // (8 // SB), (n % (8 // SB)) * SB
            kt = h * 3 + b

            def step(w, acc):
                acc = list(acc)
                for u in range(4):
                    ww = w * 4 + u
                    ar = [xr[kt, ww, p] for p in range(4)]
                    ai = [xi[kt, ww, p] for p in range(4)]
                    asum = [ar[p] + ai[p] for p in range(4)]
                    for s in range(SB):
                        br = jnp.broadcast_to(yr[kt, ww, pl.ds(s0 + s, 1)], (8, 128))
                        bi = jnp.broadcast_to(yi[kt, ww, pl.ds(s0 + s, 1)], (8, 128))
                        bd = jnp.broadcast_to(yd[kt, ww, pl.ds(s0 + s, 1)], (8, 128))
                        for p in range(4):
                            i = (s * 4 + p) * 3
                            acc[i] = acc[i] + ar[p] * br
                            acc[i + 1] = acc[i + 1] + ai[p] * bi
                            acc[i + 2] = acc[i + 2] + asum[p] * bd
                return tuple(acc)

            zero = jnp.zeros((8, 128), jnp.float32)
            acc = lax.fori_loop(0, 8, step, (zero,) * (SB * 12))
            for s in range(SB):
                sender = root * 32 + member * 8 + s0 + s
                re, im = [], []
                for p in range(4):
                    p1, p2, p3 = acc[(s * 4 + p) * 3:(s * 4 + p) * 3 + 3]
                    gap = jnp.abs(chan * 32 + p * 8 + c8 - sender)
                    keep = jnp.where((gap >= 1) & (gap <= limit), SCALE, 0.0)
                    re.append((p1 + p2) * keep)
                    im.append((p3 - p1 + p2) * keep)
                row = pl.multiple_of((s0 + s) * 32, 32)
                stack[h, b, pl.ds(row, 32), :] = jnp.concatenate(re, axis=0).astype(jnp.bfloat16)
                stack[h, 3 + b, pl.ds(row, 32), :] = jnp.concatenate(im, axis=0).astype(jnp.bfloat16)

    lhs = [jnp.concatenate([stack[h, b] for b in range(6)], axis=1) for h in range(2)]
    for n in range(3):
        cut = pl.ds(256 * n, 256)
        e = jnp.dot(lhs[0], table_ref[0, :, cut], preferred_element_type=jnp.float32)
        o = jnp.dot(lhs[1], table_ref[1, :, cut], preferred_element_type=jnp.float32)
        out_ref[0, :, pl.ds(256 * n, 256)] = (e + o).astype(jnp.bfloat16)
        out_ref[0, :, pl.ds(768 + 256 * n, 256)] = (e - o).astype(jnp.bfloat16)


def correlate(block, limit, recv, src, table):
    f32 = jnp.float32
    sm = pl.BlockSpec(memory_space=pltpu.SMEM)
    return pl.pallas_call(
        corr_kernel,
        grid=(R,),
        out_shape=jax.ShapeDtypeStruct((R, 256, 2 * F), jnp.bfloat16),
        in_specs=[
            sm, sm,
            pl.BlockSpec((4, 16, 4, 16, HALF), lambda r: (0, 0, 0, 0, 0)),
            pl.BlockSpec((2, 1, 4, 4, 2, 16, HALF), lambda r: (0, r, 0, 0, 0, 0, 0)),
            pl.BlockSpec((2, F, F), lambda r: (0, 0, 0)),
        ],
        out_specs=pl.BlockSpec((1, 256, 2 * F), lambda r: (r, 0, 0)),
        scratch_shapes=[
            pltpu.VMEM((6, 32, 4, 8, 128), f32), pltpu.VMEM((6, 32, 4, 8, 128), f32),
            pltpu.VMEM((6, 32, 8, 128), f32), pltpu.VMEM((6, 32, 8, 128), f32), pltpu.VMEM((6, 32, 8, 128), f32),
            pltpu.VMEM((2, 6, 256, 128), jnp.bfloat16),
        ],
        compiler_params=pltpu.CompilerParams(vmem_limit_bytes=50 * 2**20),
        name="correlate",
    )(block, limit, recv, src, table)


def shards(spectra, window_flags, source_block, offset_limit):
    rows, cols, table = constants()
    bf = jnp.bfloat16
    spec = spectra.reshape(2, 256, F)
    recv, src = comm(source_block, window_flags, spec, jnp.asarray(rows, bf), jnp.asarray(cols, bf))
    out = correlate(source_block, offset_limit, recv, src, jnp.asarray(table, bf))
    return out.reshape(R, 8, 32, 2 * F)


def solution(mesh):
    in_specs = (P(None, "chan", "win", None), P("win"), P(), P())
    out_specs = P(None, "win", "chan", None)
    return jax.shard_map(shards, mesh=mesh, in_specs=in_specs, out_specs=out_specs, check_vma=False)
```

time: 637 us -> 109 us (0.17)
  waiting for transfers between devices: 347 us -> 0 us
  matrix products: 141 us -> 0 us
  Pallas kernels: 0 us -> 102 us
  local copies, waits for them, and re-layouts: 82.4 us -> 6.57 us
  other arithmetic: 34.8 us -> 0 us
  between operations: 20.2 us -> 0.02 us
    psum x1 -> x0, waiting for transfers between devices: 310 us -> none  [from_root(): return lax.psum(block, axis)]
    dot_general x20 -> x0, matrix products: 141 us -> none  [the longest x4 37.1 us: shards(): jnp.einsum('scf,fl->scl', stack, table, precision=lax.Precision.HIGHEST)]
    pallas_call x0 -> x2, Pallas kernels: none -> 102 us  [the longest x1 61 us: comm(): pl.pallas_call(comm_kernel, out_shape=(jax.ShapeDtypeStruct((4, 16, 4, 16...]
    dot_general x16 -> x0, local copies, waits for them, and re-layouts: 42.5 us -> none  [the longest x4 12.9 us: cross_stack(): jnp.einsum('swf,cwf->scf', source[1], flagged[1], preferred_element_type=...]
    squeeze x13 -> x0, local copies, waits for them, and re-layouts: 37.4 us -> none  [the longest x6 9.93 us: cross_stack(): source[1]]
    all_gather x1 -> x0, waiting for transfers between devices: 36.8 us -> none  [shards(): lax.all_gather(white, 'win', axis=2, tiled=True)]
    mul x7 -> x0, other arithmetic: 23.8 us -> none  [the longest x1 20.5 us: lag_table(): weight[:, None] * jnp.cos(theta)]
  transfers between devices with their start and end apart: 2 -> 0, of which waited for: 2 -> 0; matrix products, arithmetic and copies ran while one was open for 7% -> 0% of each run, Pallas kernels for 0% -> 0%
where the time goes in v1:
time: 109 us; the launch traced here: 108 us
  Pallas kernels  102 us (94%)
  local copies, waits for them, and re-layouts  6.57 us (6%)
    pallas_call x1, Pallas kernels, comm(): pl.pallas_call(comm_kernel, out_shape=(jax.ShapeDtypeStruct((4, 16, 4, 16...  61 us
    pallas_call x1, Pallas kernels, correlate(): pl.pallas_call(corr_kernel, grid=(R,), out_shape=jax.ShapeDtypeStruct((R,...  40.8 us
    unnamed x14, local copies, waits for them, and re-layouts  6.57 us

profile of v1, /device:TPU:0, one launch (start us, length us, event | category | flops | bytes accessed | tf_op | source)
XLA Modules:
  0.0 108.4 jit_solution(9233579492132742048)
XLA Ops:
  0.0 0.0 copy-start.1
  0.0 1.1 %copy-done.1 = bf16[2,32,8,768]{3,2,1,0:T(8,128)(2,1)S(1)} copy-done((bf16[2,32,8,768]{3,2,1,0:T(8,128)(2,1)S(1)}, bf16[2,32,8,768]{3,2,1,0:T(8,128)(2,1)}, u32[]{:S(2)}) %copy-start.1) | copy-done | bytes 786456
  1.1 0.0 copy-start.2
  1.1 0.9 copy-done.2
  2.0 0.0 copy-start.3
  2.0 0.9 copy-done.3
  2.9 0.0 copy-start.4
  2.9 0.7 copy-done.4
  3.6 0.0 copy-start.5
  3.6 0.7 copy-done.5
  4.3 61.0 %comm.1 = (bf16[4,16,4,16,384]{4,3,2,1,0:T(8,128)(2,1)}, bf16[2,4,4,4,2,16,384]{6,5,4,3,2,1,0:T(8,128)(2,1)}) custom-call(s32[4]{0:T(128)S(1)} %copy-done.4, s32[8]{0:T(128)S(1)} %copy-done.5, bf16[2,256,768]{2,1,0:T(8,128)(2,1)S(1)} %bitcast.2, bf16[256,256]{1,0:T(8,128)(2,1)S(1)} %copy-done.3, bf16[256,256]{1,0:T(8,128)(2,1)S(1)} %copy-done.2), custom_call_target="tpu_custom_call" | custom-call | tf_op jit(solution)/shard_map/comm/pallas_call | solution.py:173
  65.3 0.0 copy-start
  65.3 1.7 %copy-done = bf16[2,768,768]{2,1,0:T(8,128)(2,1)S(1)} copy-done((bf16[2,768,768]{2,1,0:T(8,128)(2,1)S(1)}, bf16[2,768,768]{2,1,0:T(8,128)(2,1)}, u32[]{:S(2)}) %copy-start) | copy-done | bytes 2359320
  67.0 0.0 copy-start.6
  67.0 0.7 copy-done.6
  67.6 40.8 %correlate.1 = bf16[4,256,1536]{2,1,0:T(8,128)(2,1)} custom-call(s32[4]{0:T(128)S(1)} %copy-done.4, s32[4]{0:T(128)S(1)} %copy-done.6, bf16[4,16,4,16,384]{4,3,2,1,0:T(8,128)(2,1)} %get-tuple-element.7.recv_ref, bf16[2,4,4,4,2,16,384]{6,5,4,3,2,1,0:T(8,128)(2,1)} %get-tuple-element.8.src_ref, bf16[2,768,768]{2,1,0:T(8,128)(2,1)S(1)} %copy-done), custom_call_target="tpu_custom_call" | custom-call | tf_op jit(solution)/shard_map/correlate/pallas_call | solution.py:284
Async XLA Ops:
  0.0 1.1 %copy-start.1 = (bf16[2,32,8,768]{3,2,1,0:T(8,128)(2,1)S(1)}, bf16[2,32,8,768]{3,2,1,0:T(8,128)(2,1)}, u32[]{:S(2)}) copy-start(bf16[2,32,8,768]{3,2,1,0:T(8,128)(2,1)} %param.7) | copy-start | bytes 2359300
  1.1 0.9 copy-start.2
  2.0 0.9 copy-start.3
  2.9 0.7 copy-start.4
  3.6 0.7 copy-start.5
  65.3 1.7 %copy-start = (bf16[2,768,768]{2,1,0:T(8,128)(2,1)S(1)}, bf16[2,768,768]{2,1,0:T(8,128)(2,1)}, u32[]{:S(2)}) copy-start(bf16[2,768,768]{2,1,0:T(8,128)(2,1)} %constant.8.clone.table_ref) | copy-start | bytes 7077892
  67.0 0.7 copy-start.6

commit v2 on v1

v2 whole, which is shorter than its diff:
```python
import math

import jax
import jax.numpy as jnp
import numpy as np
from jax import lax
from jax.experimental import pallas as pl
from jax.experimental.pallas import tpu as pltpu
from jax.sharding import PartitionSpec as P

MESH = pl.DeviceIdType.MESH
F = 768
HALF = 384
R = 4
SCALE = 1.0 / math.sqrt(24576.0)


def constants():
    rows = np.zeros((256, 256), np.float32)
    for wp in range(4):
        for p in range(4):
            for w2 in range(2):
                for c in range(8):
                    rows[((wp * 4 + p) * 2 + w2) * 8 + c, (p * 8 + c) * 8 + wp * 2 + w2] = 1.0
    cols = np.zeros((256, 256), np.float32)
    for i in range(128):
        cols[2 * i, i] = 1.0
        cols[2 * i + 1, 128 + i] = 1.0
    k = (256 * np.arange(3)[:, None] + 2 * np.arange(128)[None, :]).reshape(-1)
    lag = np.arange(768) - 768
    table = np.zeros((2, 768, 768), np.float32)
    for h in range(2):
        kk = k + h
        m = (kk[:, None] * lag[None, :]) % 1536
        g = np.where(kk == 0, 1.0, 2.0)[:, None]
        table[h, :HALF] = g * np.cos(np.pi * m / 768.0)
        table[h, HALF:] = -g * np.sin(np.pi * m / 768.0)
    return rows, cols, table


def coords():
    c, w = lax.axis_index("chan"), lax.axis_index("win")
    return c // 8, (c // 2) % 4, c % 2, w


def dev(x, z, yh, j):
    return (x * 8 + z * 2 + yh, j)


def whiten_into(spec_ref, flag_ref, rows_ref, cols_ref, out):
    for wp in range(4):
        part = []
        for reim in range(2):
            moved = jnp.dot(rows_ref[pl.ds(wp * 64, 64), :], spec_ref[reim], preferred_element_type=jnp.float32)
            moved = moved.astype(jnp.bfloat16)
            cut = [
                jnp.dot(moved[:, 256 * b:256 * b + 256], cols_ref[...], preferred_element_type=jnp.float32)
                for b in range(3)
            ]
            even = jnp.concatenate([c[:, :128] for c in cut], axis=1)
            odd = jnp.concatenate([c[:, 128:] for c in cut], axis=1)
            part.append((even, odd))
        (re0, re1), (im0, im1) = part
        p0 = re0 * re0 + im0 * im0
        p1 = re1 * re1 + im1 * im1
        level = (jnp.sum(p0, axis=1, keepdims=True) + jnp.sum(p1, axis=1, keepdims=True)) * (1.0 / F)
        base = 0.25 * level + 1e-06
        row = lax.broadcasted_iota(jnp.int32, (64, 1), 0)
        f0 = flag_ref[2 * wp].astype(jnp.float32)
        f1 = flag_ref[2 * wp + 1].astype(jnp.float32)
        flag = jnp.where((row // 8) % 2 == 0, f0, f1)
        q0 = lax.rsqrt(p0 + base) * flag
        q1 = lax.rsqrt(p1 + base) * flag
        for reim, h, v in ((0, 0, re0 * q0), (0, 1, re1 * q1), (1, 0, im0 * q0), (1, 1, im1 * q1)):
            out[reim * 8 + wp * 2 + h] = v.astype(jnp.bfloat16).reshape(4, 16, HALF)


def spread_receivers(recv, xr, xi):
    @pl.loop(0, 16)
    def _(n):
        a, wp = n // 4, n % 4
        for h in range(2):
            for reim, to in ((0, xr), (1, xi)):
                for p in range(4):
                    v = recv[a, reim * 8 + wp * 2 + h, p].astype(jnp.float32)
                    for b in range(3):
                        for w2 in range(2):
                            to[h * 3 + b, n * 2 + w2, p] = v[8 * w2:8 * w2 + 8, 128 * b:128 * b + 128]


def spread_sources(src, r, yr, yi, yd):
    @pl.loop(0, 16)
    def _(n):
        a, wp = n // 4, n % 4
        for h in range(2):
            lo, hi = wp * 2 + h, 8 + wp * 2 + h
            vr = src[a // 2, r, lo // 4, lo % 4, a % 2].astype(jnp.float32)
            vi = src[a // 2, r, hi // 4, hi % 4, a % 2].astype(jnp.float32)
            for b in range(3):
                for w2 in range(2):
                    cr = vr[8 * w2:8 * w2 + 8, 128 * b:128 * b + 128]
                    ci = vi[8 * w2:8 * w2 + 8, 128 * b:128 * b + 128]
                    yr[h * 3 + b, n * 2 + w2] = cr
                    yi[h * 3 + b, n * 2 + w2] = ci
                    yd[h * 3 + b, n * 2 + w2] = cr - ci


SB = 4
UNROLL = 8


def cross_round(xr, xi, yr, yi, yd, stack, root, limit, chan, member):
    c8 = lax.broadcasted_iota(jnp.int32, (8, 1), 0)

    @pl.loop(0, 6)
    def _(kt):
        for s0 in range(0, 8, SB):
            def step(w, acc):
                acc = list(acc)
                for u in range(UNROLL):
                    ww = w * UNROLL + u
                    ar = [xr[kt, ww, p] for p in range(4)]
                    ai = [xi[kt, ww, p] for p in range(4)]
                    asum = [ar[p] + ai[p] for p in range(4)]
                    for s in range(SB):
                        br = jnp.broadcast_to(yr[kt, ww, pl.ds(s0 + s, 1)], (8, 128))
                        bi = jnp.broadcast_to(yi[kt, ww, pl.ds(s0 + s, 1)], (8, 128))
                        bd = jnp.broadcast_to(yd[kt, ww, pl.ds(s0 + s, 1)], (8, 128))
                        for p in range(4):
                            i = (s * 4 + p) * 3
                            acc[i] = acc[i] + ar[p] * br
                            acc[i + 1] = acc[i + 1] + ai[p] * bi
                            acc[i + 2] = acc[i + 2] + asum[p] * bd
                return tuple(acc)

            zero = jnp.zeros((8, 128), jnp.float32)
            acc = lax.fori_loop(0, 32 // UNROLL, step, (zero,) * (SB * 12))
            for s in range(SB):
                sender = root * 32 + member * 8 + s0 + s
                re, im = [], []
                for p in range(4):
                    p1, p2, p3 = acc[(s * 4 + p) * 3:(s * 4 + p) * 3 + 3]
                    gap = jnp.abs(chan * 32 + p * 8 + c8 - sender)
                    keep = jnp.where((gap >= 1) & (gap <= limit), SCALE, 0.0)
                    re.append((p1 + p2) * keep)
                    im.append((p3 - p1 + p2) * keep)
                row = (s0 + s) * 32
                stack[kt // 3, kt % 3, pl.ds(row, 32), :] = jnp.concatenate(re, axis=0).astype(jnp.bfloat16)
                stack[kt // 3, 3 + kt % 3, pl.ds(row, 32), :] = jnp.concatenate(im, axis=0).astype(jnp.bfloat16)


def lag_round(stack, table, out, r):
    lhs = [jnp.concatenate([stack[h, b] for b in range(6)], axis=1) for h in range(2)]
    for n in range(3):
        cut = pl.ds(256 * n, 256)
        e = jnp.dot(lhs[0], table[0, :, cut], preferred_element_type=jnp.float32)
        o = jnp.dot(lhs[1], table[1, :, cut], preferred_element_type=jnp.float32)
        out[r, :, pl.ds(256 * n, 256)] = (e + o).astype(jnp.bfloat16)
        out[r, :, pl.ds(768 + 256 * n, 256)] = (e - o).astype(jnp.bfloat16)


def kernel(block_ref, limit_ref, flag_ref, spec_hbm, rows_hbm, cols_hbm, table_hbm, out_hbm,
           spec, rows, cols, table, recv, cand, pick, diag, src, xr, xi, yr, yi, yd, stack, out,
           a_s, a_r, d_s, d_r, p_s, p_r, g_s, g_r, f_s, f_r, i_s, o_s, t_s, t_r, u_s, u_r):
    x, z, yh, j = coords()
    slot = x * 4 + z
    bar = pltpu.get_barrier_semaphore()
    plane = []
    for t in range(1, 16):
        to = (slot + t) % 16
        plane.append((to, dev(to // 4, to % 4, yh, j)))
    column = []
    for t in range(1, 8):
        column.append((t, (j + t) % 4, dev(x, z, (yh + t // 4) % 2, (j + t) % 4)))
    loads = [
        pltpu.make_async_copy(s, d, i_s.at[n])
        for n, (s, d) in enumerate(((spec_hbm, spec), (rows_hbm, rows), (cols_hbm, cols), (table_hbm, table)))
    ]
    for c in loads:
        c.start()
    for _, d in plane:
        pl.semaphore_signal(bar, inc=1, device_id=d, device_id_type=MESH)
    for _, _, d in column:
        pl.semaphore_signal(bar, inc=1, device_id=d, device_id_type=MESH)

    for c in loads[:3]:
        c.wait()
    whiten_into(spec, flag_ref, rows, cols, recv.at[j])
    pl.semaphore_wait(bar, 22)
    sends = []

    def remote(s, d, ss, rs, to):
        return pltpu.make_async_remote_copy(
            src_ref=s, dst_ref=d, send_sem=ss, recv_sem=rs, device_id=to, device_id_type=MESH)

    def send(*args):
        c = remote(*args)
        c.start()
        sends.append(c)
        return c

    mate = dev(x, z, yh, j + 1 - 2 * (j % 2))
    across = (j + 2) % 4
    other = dev(x, z, yh, across)
    swap = [send(recv.at[j, to], cand.at[slot], a_s.at[t], a_r.at[t], d) for t, (to, d) in enumerate(plane)]
    over = [
        send(recv.at[j, pl.ds(4 * q, 4)], recv.at[j, pl.ds(4 * q, 4)], g_s.at[q], g_r.at[q], other)
        for q in range(4)
    ]
    to_mate = send(recv.at[j], recv.at[j], p_s.at[0], p_r.at[0], mate)
    cand[slot] = recv[j, slot]

    relayed = []

    def relay(q):
        over[q].wait_recv()
        relayed.append(send(recv.at[across, pl.ds(4 * q, 4)], recv.at[across, pl.ds(4 * q, 4)], f_s.at[q], f_r.at[q], mate))

    for c in swap:
        c.wait_recv()
    for r in range(R):
        pick[:, r] = cand[block_ref[r] // 2]
    meet = [send(pick.at[p], diag.at[yh, j], d_s.at[t], d_r.at[t], d) for t, p, d in column]
    diag[yh, j] = pick[j]
    relay(0)
    for c in meet:
        c.wait_recv()
    first = []
    for r in range(R):
        got = diag[block_ref[r] % 2, :, r]
        src[0, r, x, z] = got[0:2]
        src[1, r, x, z] = got[2:4]
        one = []
        for d in range(1, 4):
            z2, x2 = (z + d) % 4, (x + d) % 4
            one.append(send(src.at[0, r, x, z], src.at[0, r, x, z], t_s.at[0, r, d], t_r.at[0, r, d], dev(x, z2, yh, j)))
            one.append(send(src.at[1, r, x, z], src.at[1, r, x, z], t_s.at[1, r, d], t_r.at[1, r, d], dev(x2, z, yh, j)))
        first.append(one)
    relay(1)

    def spread(r, d):
        z2, x2 = (z + d) % 4, (x + d) % 4
        return (
            remote(src.at[0, r, x], src.at[0, r, x], u_s.at[0, r, d], u_r.at[0, r, d], dev(x2, z, yh, j)),
            remote(src.at[1, r, :, z], src.at[1, r, :, z], u_s.at[1, r, d], u_r.at[1, r, d], dev(x, z2, yh, j)),
        )

    for r in range(R):
        for c in first[r]:
            c.wait_recv()
        for d in range(1, 4):
            for c in spread(r, d):
                c.start()
    relay(2)
    relay(3)
    to_mate.wait_recv()
    for c in relayed:
        c.wait_recv()
    spread_receivers(recv, xr, xi)
    loads[3].wait()
    chan = x * 8 + z * 2 + yh

    @pl.loop(0, R)
    def _(r):
        for d in range(1, 4):
            for c in spread(r, d):
                c.wait_recv()
        spread_sources(src, r, yr, yi, yd)
        cross_round(xr, xi, yr, yi, yd, stack, block_ref[r], limit_ref[r], chan, j)
        lag_round(stack, table, out, r)
        pltpu.make_async_copy(out.at[r], out_hbm.at[r], o_s.at[r]).start()

    for r in range(R):
        pltpu.make_async_copy(out.at[r], out_hbm.at[r], o_s.at[r]).wait()
        for d in range(1, 4):
            for c in spread(r, d):
                c.wait_send()
    for c in sends:
        c.wait_send()


def fused(block, limit, flags, spec, rows, cols, table):
    bf, f32 = jnp.bfloat16, jnp.float32
    dma = pltpu.SemaphoreType.DMA
    hbm = pl.BlockSpec(memory_space=pl.ANY)
    sm = pl.BlockSpec(memory_space=pltpu.SMEM)
    vm = pltpu.VMEM
    return pl.pallas_call(
        kernel,
        out_shape=jax.ShapeDtypeStruct((R, 256, 2 * F), bf),
        in_specs=[sm, sm, sm, hbm, hbm, hbm, hbm],
        out_specs=hbm,
        scratch_shapes=[
            vm((2, 256, F), bf), vm((256, 256), bf), vm((256, 256), bf), vm((2, F, F), bf),
            vm((4, 16, 4, 16, HALF), bf),
            vm((16, 4, 16, HALF), bf),
            vm((4, R, 16, HALF), bf),
            vm((2, 4, R, 16, HALF), bf),
            vm((2, R, 4, 4, 2, 16, HALF), bf),
            vm((6, 32, 4, 8, 128), f32), vm((6, 32, 4, 8, 128), f32),
            vm((6, 32, 8, 128), f32), vm((6, 32, 8, 128), f32), vm((6, 32, 8, 128), f32),
            vm((2, 6, 256, 128), bf),
            vm((R, 256, 2 * F), bf),
            dma((16,)), dma((16,)), dma((8,)), dma((8,)), dma((1,)), dma((1,)),
            dma((4,)), dma((4,)), dma((4,)), dma((4,)), dma((4,)), dma((4,)),
            dma((2, R, 4)), dma((2, R, 4)), dma((2, R, 4)), dma((2, R, 4)),
        ],
        compiler_params=pltpu.CompilerParams(
            collective_id=1, has_side_effects=True, vmem_limit_bytes=56 * 2**20),
        name="whiten_correlate",
    )(block, limit, flags, spec, rows, cols, table)


def shards(spectra, window_flags, source_block, offset_limit):
    rows, cols, table = (jnp.asarray(v, jnp.bfloat16) for v in constants())
    spec = spectra.reshape(2, 256, F)
    out = fused(source_block, offset_limit, window_flags, spec, rows, cols, table)
    return out.reshape(R, 8, 32, 2 * F)


def solution(mesh):
    in_specs = (P(None, "chan", "win", None), P("win"), P(), P())
    out_specs = P(None, "win", "chan", None)
    return jax.shard_map(shards, mesh=mesh, in_specs=in_specs, out_specs=out_specs, check_vma=False)
```

time: 109 us -> 82.9 us (0.76)
  Pallas kernels: 102 us -> 78.9 us
  local copies, waits for them, and re-layouts: 6.57 us -> 3.88 us
    pallas_call x2 -> x1, Pallas kernels: 102 us -> 78.9 us  [fused(): pl.pallas_call(kernel, out_shape=jax.ShapeDtypeStruct((R, 256, 2 * F), bf...]
    unnamed x14 -> x1, local copies, waits for them, and re-layouts: 6.57 us -> 3.88 us
where the time goes in v2:
time: 82.9 us; the launch traced here: 82.8 us
  Pallas kernels  78.9 us (95%)
  local copies, waits for them, and re-layouts  3.88 us (5%)
    pallas_call x1, Pallas kernels, fused(): pl.pallas_call(kernel, out_shape=jax.ShapeDtypeStruct((R, 256, 2 * F), bf...  78.9 us
    unnamed x1, local copies, waits for them, and re-layouts  3.88 us

profile of v2, /device:TPU:0, one launch (start us, length us, event | category | flops | bytes accessed | tf_op | source)
XLA Modules:
  0.0 82.8 jit_solution(6265023478247422165)
XLA Ops:
  0.0 78.9 %whiten_correlate.1 = bf16[4,256,1536]{2,1,0:T(8,128)(2,1)} custom-call(s32[4]{0:T(128)} %block_ref.1, s32[4]{0:T(128)} %limit_ref.1, s32[8]{0:T(128)} %flag_ref.1, bf16[2,256,768]{2,1,0:T(8,128)(2,1)} %bitcast.3, bf16[256,256]{1,0:T(8,128)(2,1)} %constant.6.clone.rows_hbm, bf16[256,256]{1,0:T(8,128)(2,1)} %constant.7.clone.cols_hbm, ...), custom_call_target="tpu_custom_call" | custom-call | tf_op jit(solution)/shard_map/whiten_correlate/pallas_call | solution.py:288
  78.9 3.9 %copy.9 = bf16[4,8,32,1536]{3,2,1,0:T(8,128)(2,1)} copy(bf16[4,8,32,1536]{3,2,1,0:T(8,128)(2,1)} %bitcast.2) | data formatting | bytes 6291456

commit v3 on v2

v3 whole, which is shorter than its diff:
```python
import math

import jax
import jax.numpy as jnp
import numpy as np
from jax import lax
from jax.experimental import pallas as pl
from jax.experimental.pallas import tpu as pltpu
from jax.sharding import PartitionSpec as P

MESH = pl.DeviceIdType.MESH
F = 768
HALF = 384
R = 4
SCALE = 1.0 / math.sqrt(24576.0)


def constants():
    rows = np.zeros((256, 256), np.float32)
    for wp in range(4):
        for p in range(4):
            for w2 in range(2):
                for c in range(8):
                    rows[((wp * 4 + p) * 2 + w2) * 8 + c, (p * 8 + c) * 8 + wp * 2 + w2] = 1.0
    cols = np.zeros((256, 256), np.float32)
    for i in range(128):
        cols[2 * i, i] = 1.0
        cols[2 * i + 1, 128 + i] = 1.0
    k = (256 * np.arange(3)[:, None] + 2 * np.arange(128)[None, :]).reshape(-1)
    lag = np.arange(768) - 768
    table = np.zeros((2, 768, 768), np.float32)
    for h in range(2):
        kk = k + h
        m = (kk[:, None] * lag[None, :]) % 1536
        g = np.where(kk == 0, 1.0, 2.0)[:, None]
        table[h, :HALF] = g * np.cos(np.pi * m / 768.0)
        table[h, HALF:] = -g * np.sin(np.pi * m / 768.0)
    return rows, cols, table


def coords():
    c, w = lax.axis_index("chan"), lax.axis_index("win")
    return c // 8, (c // 2) % 4, c % 2, w


def dev(x, z, yh, j):
    return (x * 8 + z * 2 + yh, j)


def whiten_into(spec_ref, flag_ref, rows_ref, cols_ref, out):
    for wp in range(4):
        part = []
        for reim in range(2):
            moved = jnp.dot(rows_ref[pl.ds(wp * 64, 64), :], spec_ref[reim], preferred_element_type=jnp.float32)
            moved = moved.astype(jnp.bfloat16)
            cut = [
                jnp.dot(moved[:, 256 * b:256 * b + 256], cols_ref[...], preferred_element_type=jnp.float32)
                for b in range(3)
            ]
            even = jnp.concatenate([c[:, :128] for c in cut], axis=1)
            odd = jnp.concatenate([c[:, 128:] for c in cut], axis=1)
            part.append((even, odd))
        (re0, re1), (im0, im1) = part
        p0 = re0 * re0 + im0 * im0
        p1 = re1 * re1 + im1 * im1
        level = (jnp.sum(p0, axis=1, keepdims=True) + jnp.sum(p1, axis=1, keepdims=True)) * (1.0 / F)
        base = 0.25 * level + 1e-06
        row = lax.broadcasted_iota(jnp.int32, (64, 1), 0)
        f0 = flag_ref[2 * wp].astype(jnp.float32)
        f1 = flag_ref[2 * wp + 1].astype(jnp.float32)
        flag = jnp.where((row // 8) % 2 == 0, f0, f1)
        q0 = lax.rsqrt(p0 + base) * flag
        q1 = lax.rsqrt(p1 + base) * flag
        for reim, h, v in ((0, 0, re0 * q0), (0, 1, re1 * q1), (1, 0, im0 * q0), (1, 1, im1 * q1)):
            v = v.astype(jnp.bfloat16).reshape(4, 16, HALF)
            for b in range(3):
                out[b, reim * 8 + wp * 2 + h] = v[:, :, 128 * b:128 * b + 128]


def spread_receivers(recv, b, xr, xi, xs):
    @pl.loop(0, 4)
    def _(a):
        for wp in range(4):
            n = a * 4 + wp
            for h in range(2):
                for p in range(4):
                    re = recv[a, b, wp * 2 + h, p].astype(jnp.float32)
                    im = recv[a, b, 8 + wp * 2 + h, p].astype(jnp.float32)
                    for w2 in range(2):
                        cut = slice(8 * w2, 8 * w2 + 8)
                        xr[h, n * 2 + w2, p] = re[cut]
                        xi[h, n * 2 + w2, p] = im[cut]
                        xs[h, n * 2 + w2, p] = re[cut] + im[cut]


def spread_sources(src, b, r, yr, yi, yd):
    for n in range(16):
        a, wp = n // 4, n % 4
        for h in range(2):
            lo, hi = wp * 2 + h, 8 + wp * 2 + h
            vr = src[b, a // 2, r, lo // 4, lo % 4, a % 2].astype(jnp.float32)
            vi = src[b, a // 2, r, hi // 4, hi % 4, a % 2].astype(jnp.float32)
            for w2 in range(2):
                cr = vr[8 * w2:8 * w2 + 8]
                ci = vi[8 * w2:8 * w2 + 8]
                yr[h, n * 2 + w2] = cr
                yi[h, n * 2 + w2] = ci
                yd[h, n * 2 + w2] = cr - ci


VMEM = 56 * 2**20
SB = 4
UNROLL = 8


def cross_round(xr, xi, xs, yr, yi, yd, stack, r, b, root, limit, chan, member):
    c8 = lax.broadcasted_iota(jnp.int32, (8, 1), 0)

    @pl.loop(0, 2)
    def _(h):
        for s0 in range(0, 8, SB):
            def step(w, acc):
                acc = list(acc)
                for u in range(UNROLL):
                    ww = w * UNROLL + u
                    ar = [xr[h, ww, p] for p in range(4)]
                    ai = [xi[h, ww, p] for p in range(4)]
                    asum = [xs[h, ww, p] for p in range(4)]
                    for s in range(SB):
                        br = jnp.broadcast_to(yr[h, ww, pl.ds(s0 + s, 1)], (8, 128))
                        bi = jnp.broadcast_to(yi[h, ww, pl.ds(s0 + s, 1)], (8, 128))
                        bd = jnp.broadcast_to(yd[h, ww, pl.ds(s0 + s, 1)], (8, 128))
                        for p in range(4):
                            i = (s * 4 + p) * 3
                            acc[i] = acc[i] + ar[p] * br
                            acc[i + 1] = acc[i + 1] + ai[p] * bi
                            acc[i + 2] = acc[i + 2] + asum[p] * bd
                return tuple(acc)

            zero = jnp.zeros((8, 128), jnp.float32)
            acc = lax.fori_loop(0, 32 // UNROLL, step, (zero,) * (SB * 12))
            for s in range(SB):
                sender = root * 32 + member * 8 + s0 + s
                re, im = [], []
                for p in range(4):
                    p1, p2, p3 = acc[(s * 4 + p) * 3:(s * 4 + p) * 3 + 3]
                    gap = jnp.abs(chan * 32 + p * 8 + c8 - sender)
                    keep = jnp.where((gap >= 1) & (gap <= limit), SCALE, 0.0)
                    re.append((p1 + p2) * keep)
                    im.append((p3 - p1 + p2) * keep)
                row = (s0 + s) * 32
                stack[b, r, h, 0, pl.ds(row, 32), :] = jnp.concatenate(re, axis=0).astype(jnp.bfloat16)
                stack[b, r, h, 1, pl.ds(row, 32), :] = jnp.concatenate(im, axis=0).astype(jnp.bfloat16)


def kernel(block_ref, limit_ref, flag_ref, spec_hbm, rows_hbm, cols_hbm, out_hbm,
           spec, rows, cols, recv, cand0, cand1, cand2, pick, diag0, diag1, diag2, src, xr, xi, xs, yr, yi, yd, stack,
           a_s, a_r, d_s, d_r, p_s, p_r, g_s, g_r, f_s, f_r, i_s, o_s, t_s, t_r, u_s, u_r):
    x, z, yh, j = coords()
    slot = x * 4 + z
    cand, diag = (cand0, cand1, cand2), (diag0, diag1, diag2)
    bar = pltpu.get_barrier_semaphore()
    plane = []
    for t in range(1, 16):
        to = (slot + t) % 16
        plane.append((to, dev(to // 4, to % 4, yh, j)))
    column = []
    for t in range(1, 8):
        column.append((t, (j + t) % 4, dev(x, z, (yh + t // 4) % 2, (j + t) % 4)))
    loads = [
        pltpu.make_async_copy(s, d, i_s.at[n])
        for n, (s, d) in enumerate(((spec_hbm, spec), (rows_hbm, rows), (cols_hbm, cols)))
    ]
    for c in loads:
        c.start()
    for _, d in plane:
        pl.semaphore_signal(bar, inc=1, device_id=d, device_id_type=MESH)
    for _, _, d in column:
        pl.semaphore_signal(bar, inc=1, device_id=d, device_id_type=MESH)

    for c in loads:
        c.wait()
    whiten_into(spec, flag_ref, rows, cols, recv.at[j])
    pl.semaphore_wait(bar, 22)
    sends = []

    def remote(s, d, ss, rs, to):
        return pltpu.make_async_remote_copy(
            src_ref=s, dst_ref=d, send_sem=ss, recv_sem=rs, device_id=to, device_id_type=MESH)

    def send(*args):
        c = remote(*args)
        c.start()
        sends.append(c)
        return c

    mate = dev(x, z, yh, j + 1 - 2 * (j % 2))
    across = (j + 2) % 4
    other = dev(x, z, yh, across)
    swap = []

    def exchange(b):
        swap.append([
            send(recv.at[j, b, to], cand[b].at[slot], a_s.at[b, t], a_r.at[b, t], d)
            for t, (to, d) in enumerate(plane)
        ])

    exchange(0)
    over = []

    def cross_over(b):
        over.append(send(recv.at[j, b], recv.at[j, b], g_s.at[b], g_r.at[b], other))

    cross_over(0)
    to_mate = [send(recv.at[j, b], recv.at[j, b], p_s.at[b], p_r.at[b], mate) for b in range(3)]
    for b in range(3):
        cand[b][slot] = recv[j, b, slot]

    def relay(b):
        over[b].wait_recv()
        return send(recv.at[across, b], recv.at[across, b], f_s.at[b], f_r.at[b], mate)

    def choose(b):
        for c in swap[b]:
            c.wait_recv()
        for r in range(R):
            pick[b, :, r] = cand[b][block_ref[r] // 2]
        diag[b][yh, j] = pick[b, j]
        return [send(pick.at[b, p], diag[b].at[yh, j], d_s.at[b, t], d_r.at[b, t], d) for t, p, d in column]

    def gather(b, meet):
        for c in meet:
            c.wait_recv()
        for r in range(R):
            got = diag[b][block_ref[r] % 2, :, r]
            src[b, 0, r, x, z] = got[0:2]
            src[b, 1, r, x, z] = got[2:4]
        out = []
        for d in range(1, 4):
            z2, x2 = (z + d) % 4, (x + d) % 4
            out.append(send(src.at[b, 0, :, x, z], src.at[b, 0, :, x, z], t_s.at[b, 0, d], t_r.at[b, 0, d], dev(x, z2, yh, j)))
            out.append(send(src.at[b, 1, :, x, z], src.at[b, 1, :, x, z], t_s.at[b, 1, d], t_r.at[b, 1, d], dev(x2, z, yh, j)))
        return out

    def spread(b, r, d):
        z2, x2 = (z + d) % 4, (x + d) % 4
        return (
            remote(src.at[b, 0, r, x], src.at[b, 0, r, x], u_s.at[b, 0, r, d], u_r.at[b, 0, r, d], dev(x2, z, yh, j)),
            remote(src.at[b, 1, r, :, z], src.at[b, 1, r, :, z], u_s.at[b, 1, r, d], u_r.at[b, 1, r, d], dev(x, z2, yh, j)),
        )

    def scatter(b, first, rounds):
        for c in first:
            c.wait_recv()
        for r in rounds:
            for d in range(1, 4):
                for c in spread(b, r, d):
                    c.start()

    chan = x * 8 + z * 2 + yh
    relayed = []

    def receivers(b):
        to_mate[b].wait_recv()
        relayed[b].wait_recv()
        spread_receivers(recv, b, xr, xi, xs)

    def arrived(b, r):
        for d in range(1, 4):
            for c in spread(b, r, d):
                c.wait_recv()

    def compute(b, r):
        spread_sources(src, b, r, yr, yi, yd)
        cross_round(xr, xi, xs, yr, yi, yd, stack, r, b, block_ref[r], limit_ref[r], chan, j)
        pltpu.make_async_copy(stack.at[b, r], out_hbm.at[b, r], o_s.at[b, r]).start()

    swap[0].pop(0).wait_recv()
    exchange(1)
    m0 = choose(0)
    exchange(2)
    cross_over(1)
    m1 = choose(1)
    f0 = gather(0, m0)
    cross_over(2)
    relayed.append(relay(0))
    m2 = choose(2)
    scatter(0, f0, (0, 1))
    f1 = gather(1, m1)
    f2 = gather(2, m2)
    relayed.append(relay(1))
    receivers(0)
    arrived(0, 0)
    scatter(0, (), (2, 3))
    compute(0, 0)
    scatter(1, f1, range(R))
    arrived(0, 1)
    compute(0, 1)
    scatter(2, f2, range(R))
    relayed.append(relay(2))

    @pl.loop(2, R)
    def _(r):
        arrived(0, r)
        compute(0, r)

    for b in (1, 2):
        receivers(b)

        @pl.loop(0, R)
        def _(r):
            arrived(b, r)
            compute(b, r)

    for r in range(R):
        for b in range(3):
            pltpu.make_async_copy(stack.at[b, r], out_hbm.at[b, r], o_s.at[b, r]).wait()
            for d in range(1, 4):
                for c in spread(b, r, d):
                    c.wait_send()
    for c in sends:
        c.wait_send()


def fused(block, limit, flags, spec, rows, cols):
    bf, f32 = jnp.bfloat16, jnp.float32
    dma = pltpu.SemaphoreType.DMA
    hbm = pl.BlockSpec(memory_space=pl.ANY)
    sm = pl.BlockSpec(memory_space=pltpu.SMEM)
    vm = pltpu.VMEM
    return pl.pallas_call(
        kernel,
        out_shape=jax.ShapeDtypeStruct((3, R, 2, 2, 256, 128), bf),
        in_specs=[sm, sm, sm, hbm, hbm, hbm],
        out_specs=hbm,
        scratch_shapes=[
            vm((2, 256, F), bf), vm((256, 256), bf), vm((256, 256), bf),
            vm((4, 3, 16, 4, 16, 128), bf),
            vm((16, 4, 16, 128), bf), vm((16, 4, 16, 128), bf), vm((16, 4, 16, 128), bf),
            vm((3, 4, R, 16, 128), bf),
            vm((2, 4, R, 16, 128), bf), vm((2, 4, R, 16, 128), bf), vm((2, 4, R, 16, 128), bf),
            vm((3, 2, R, 4, 4, 2, 16, 128), bf),
            vm((2, 32, 4, 8, 128), f32), vm((2, 32, 4, 8, 128), f32), vm((2, 32, 4, 8, 128), f32),
            vm((2, 32, 8, 128), f32), vm((2, 32, 8, 128), f32), vm((2, 32, 8, 128), f32),
            vm((3, R, 2, 2, 256, 128), bf),
            dma((3, 16)), dma((3, 16)), dma((3, 8)), dma((3, 8)), dma((3,)), dma((3,)),
            dma((3,)), dma((3,)), dma((3,)), dma((3,)), dma((3,)), dma((3, R)),
            dma((3, 2, 4)), dma((3, 2, 4)), dma((3, 2, R, 4)), dma((3, 2, R, 4)),
        ],
        compiler_params=pltpu.CompilerParams(
            collective_id=1, has_side_effects=True, vmem_limit_bytes=VMEM),
        name="whiten_correlate",
    )(block, limit, flags, spec, rows, cols)


def lag_kernel(stack, table, out):
    lhs = [jnp.concatenate([stack[b, 0, h, q] for q in range(2) for b in range(3)], axis=1) for h in range(2)]
    for n in range(3):
        cut = pl.ds(256 * n, 256)
        e = jnp.dot(lhs[0], table[0, :, cut], preferred_element_type=jnp.float32)
        o = jnp.dot(lhs[1], table[1, :, cut], preferred_element_type=jnp.float32)
        out[0, :, pl.ds(256 * n, 256)] = (e + o).astype(jnp.bfloat16)
        out[0, :, pl.ds(768 + 256 * n, 256)] = (e - o).astype(jnp.bfloat16)


def lags(stack, table):
    return pl.pallas_call(
        lag_kernel,
        grid=(R,),
        out_shape=jax.ShapeDtypeStruct((R, 256, 2 * F), jnp.bfloat16),
        in_specs=[
            pl.BlockSpec((3, 1, 2, 2, 256, 128), lambda r: (0, r, 0, 0, 0, 0)),
            pl.BlockSpec((2, F, F), lambda r: (0, 0, 0)),
        ],
        out_specs=pl.BlockSpec((1, 256, 2 * F), lambda r: (r, 0, 0)),
        compiler_params=pltpu.CompilerParams(vmem_limit_bytes=24 * 2**20),
        name="lag_product",
    )(stack, table)


def shards(spectra, window_flags, source_block, offset_limit):
    rows, cols, table = (jnp.asarray(v, jnp.bfloat16) for v in constants())
    spec = spectra.reshape(2, 256, F)
    stack = fused(source_block, offset_limit, window_flags, spec, rows, cols)
    out = lags(stack, table)
    return out.reshape(R, 8, 32, 2 * F)


def solution(mesh):
    in_specs = (P(None, "chan", "win", None), P("win"), P(), P())
    out_specs = P(None, "win", "chan", None)
    return jax.shard_map(shards, mesh=mesh, in_specs=in_specs, out_specs=out_specs, check_vma=False)
```

time: 82.9 us -> 73.2 us (0.88)
  Pallas kernels: 78.9 us -> 71.2 us
  local copies, waits for them, and re-layouts: 3.88 us -> 1.89 us
    pallas_call x1 -> x2, Pallas kernels: 78.9 us -> 71.2 us  [the longest x1 66.9 us: fused(): pl.pallas_call(kernel, out_shape=jax.ShapeDtypeStruct((3, R, 2, 2, 256, 1...]
    unnamed x1 -> x4, local copies, waits for them, and re-layouts: 3.88 us -> 1.89 us
where the time goes in v3:
time: 73.2 us; the launch traced here: 73.1 us
  Pallas kernels  71.2 us (97%)
  local copies, waits for them, and re-layouts  1.89 us (3%)
    pallas_call x1, Pallas kernels, fused(): pl.pallas_call(kernel, out_shape=jax.ShapeDtypeStruct((3, R, 2, 2, 256, 1...  66.9 us
    pallas_call x1, Pallas kernels, lags(): pl.pallas_call(lag_kernel, grid=(R,), out_shape=jax.ShapeDtypeStruct((R,...  4.28 us
    unnamed x4, local copies, waits for them, and re-layouts  1.89 us

profile of v3, /device:TPU:0, one launch (start us, length us, event | category | flops | bytes accessed | tf_op | source)
XLA Modules:
  0.0 73.1 jit_solution(59702047893178429)
XLA Ops:
  0.0 0.0 copy-start.1
  0.0 66.9 %whiten_correlate.1.stack = bf16[3,4,2,2,256,128]{5,4,3,2,1,0:T(8,128)(2,1)} custom-call(s32[4]{0:T(128)} %block_ref.1, s32[4]{0:T(128)} %limit_ref.1, s32[8]{0:T(128)} %flag_ref.1, bf16[2,256,768]{2,1,0:T(8,128)(2,1)} %bitcast.2, bf16[256,256]{1,0:T(8,128)(2,1)} %constant.6.clone.rows_hbm, bf16[256,256]{1,0:T(8,128)(2,1)} %constant.7.clone.cols_hbm), custom_call_target="tpu_custom_call" | custom-call | tf_op jit(solution)/shard_map/whiten_correlate/pallas_call | solution.py:331
  66.9 0.0 copy-done.1
  66.9 0.0 copy-start
  66.9 1.9 %copy-done = bf16[3,4,2,2,256,128]{5,4,3,2,1,0:T(8,128)(2,1)S(1)} copy-done((bf16[3,4,2,2,256,128]{5,4,3,2,1,0:T(8,128)(2,1)S(1)}, bf16[3,4,2,2,256,128]{5,4,3,2,1,0:T(8,128)(2,1)}, u32[]{:S(2)}) %copy-start) | copy-done | bytes 3145752
  68.8 4.3 %lag_product.1 = bf16[4,256,1536]{2,1,0:T(8,128)(2,1)} custom-call(bf16[3,4,2,2,256,128]{5,4,3,2,1,0:T(8,128)(2,1)S(1)} %copy-done, bf16[2,768,768]{2,1,0:T(8,128)(2,1)S(1)} %copy-done.1), custom_call_target="tpu_custom_call" | custom-call | tf_op jit(solution)/shard_map/lag_product/pallas_call | solution.py:367
Async XLA Ops:
  0.0 66.9 %copy-start.1 = (bf16[2,768,768]{2,1,0:T(8,128)(2,1)S(1)}, bf16[2,768,768]{2,1,0:T(8,128)(2,1)}, u32[]{:S(2)}) copy-start(bf16[2,768,768]{2,1,0:T(8,128)(2,1)} %constant.8.clone.table) | copy-start | bytes 7077892
  66.9 1.9 %copy-start = (bf16[3,4,2,2,256,128]{5,4,3,2,1,0:T(8,128)(2,1)S(1)}, bf16[3,4,2,2,256,128]{5,4,3,2,1,0:T(8,128)(2,1)}, u32[]{:S(2)}) copy-start(bf16[3,4,2,2,256,128]{5,4,3,2,1,0:T(8,128)(2,1)} %whiten_correlate.1.stack) | copy-start | bytes 9437188

commit v4 on v3

--- a/solution.py
+++ b/solution.py
@@ -110,7 +110,7 @@
 
 VMEM = 56 * 2**20
 SB = 4
-UNROLL = 8
+UNROLL = 32
 
 
 def cross_round(xr, xi, xs, yr, yi, yd, stack, r, b, root, limit, chan, member):
@@ -353,27 +353,48 @@
     )(block, limit, flags, spec, rows, cols)
 
 
-def lag_kernel(stack, table, out):
-    lhs = [jnp.concatenate([stack[b, 0, h, q] for q in range(2) for b in range(3)], axis=1) for h in range(2)]
-    for n in range(3):
-        cut = pl.ds(256 * n, 256)
-        e = jnp.dot(lhs[0], table[0, :, cut], preferred_element_type=jnp.float32)
-        o = jnp.dot(lhs[1], table[1, :, cut], preferred_element_type=jnp.float32)
-        out[0, :, pl.ds(256 * n, 256)] = (e + o).astype(jnp.bfloat16)
-        out[0, :, pl.ds(768 + 256 * n, 256)] = (e - o).astype(jnp.bfloat16)
+def lag_kernel(stack_hbm, table_hbm, out_hbm, stack, table, out, s_sem, t_sem, o_sem):
+    takes = [pltpu.make_async_copy(stack_hbm.at[:, r], stack.at[r], s_sem.at[r]) for r in range(R)]
+    cols = [
+        pltpu.make_async_copy(table_hbm.at[:, :, pl.ds(256 * n, 256)], table.at[n], t_sem.at[n]) for n in range(3)
+    ]
+    takes[0].start()
+    for c in cols:
+        c.start()
+    for c in takes[1:]:
+        c.start()
+    puts = []
+    for r in range(R):
+        takes[r].wait()
+        lhs = [jnp.concatenate([stack[r, b, h, q] for q in range(2) for b in range(3)], axis=1) for h in range(2)]
+        for n in range(3):
+            if r == 0:
+                cols[n].wait()
+            e = jnp.dot(lhs[0], table[n, 0], preferred_element_type=jnp.float32)
+            o = jnp.dot(lhs[1], table[n, 1], preferred_element_type=jnp.float32)
+            out[r, :, pl.ds(256 * n, 256)] = (e + o).astype(jnp.bfloat16)
+            out[r, :, pl.ds(768 + 256 * n, 256)] = (e - o).astype(jnp.bfloat16)
+        puts.append(pltpu.make_async_copy(out.at[r], out_hbm.at[r], o_sem.at[r]))
+        puts[-1].start()
+    for c in puts:
+        c.wait()
 
 
 def lags(stack, table):
+    bf, dma = jnp.bfloat16, pltpu.SemaphoreType.DMA
+    hbm = pl.BlockSpec(memory_space=pl.ANY)
     return pl.pallas_call(
         lag_kernel,
-        grid=(R,),
-        out_shape=jax.ShapeDtypeStruct((R, 256, 2 * F), jnp.bfloat16),
-        in_specs=[
-            pl.BlockSpec((3, 1, 2, 2, 256, 128), lambda r: (0, r, 0, 0, 0, 0)),
-            pl.BlockSpec((2, F, F), lambda r: (0, 0, 0)),
+        out_shape=jax.ShapeDtypeStruct((R, 256, 2 * F), bf),
+        in_specs=[hbm, hbm],
+        out_specs=hbm,
+        scratch_shapes=[
+            pltpu.VMEM((R, 3, 2, 2, 256, 128), bf),
+            pltpu.VMEM((3, 2, F, 256), bf),
+            pltpu.VMEM((R, 256, 2 * F), bf),
+            dma((R,)), dma((3,)), dma((R,)),
         ],
-        out_specs=pl.BlockSpec((1, 256, 2 * F), lambda r: (r, 0, 0)),
-        compiler_params=pltpu.CompilerParams(vmem_limit_bytes=24 * 2**20),
+        compiler_params=pltpu.CompilerParams(vmem_limit_bytes=60 * 2**20),
         name="lag_product",
     )(stack, table)
 

time: 73.2 us -> 70.9 us (0.969)
  local copies, waits for them, and re-layouts: 1.89 us -> 0 us
    pallas_call x1, Pallas kernels: 66.9 us -> 64.7 us  [fused(): pl.pallas_call(kernel, out_shape=jax.ShapeDtypeStruct((3, R, 2, 2, 256, 1...]
    unnamed x4 -> x0, local copies, waits for them, and re-layouts: 1.89 us -> none
    pallas_call x1, Pallas kernels: 4.28 us -> 6.04 us  [lags(): pl.pallas_call(lag_kernel, out_shape=jax.ShapeDtypeStruct((R, 256, 2 * F)...]
where the time goes in v4:
time: 70.9 us; the launch traced here: 70.7 us
  Pallas kernels  70.7 us (100%)
    pallas_call x1, Pallas kernels, fused(): pl.pallas_call(kernel, out_shape=jax.ShapeDtypeStruct((3, R, 2, 2, 256, 1...  64.7 us
    pallas_call x1, Pallas kernels, lags(): pl.pallas_call(lag_kernel, out_shape=jax.ShapeDtypeStruct((R, 256, 2 * F)...  6.04 us

profile of v4, /device:TPU:0, one launch (start us, length us, event | category | flops | bytes accessed | tf_op | source)
XLA Modules:
  0.0 70.7 jit_solution(5145557238450037586)
XLA Ops:
  0.0 64.7 %whiten_correlate.1.stack_hbm = bf16[3,4,2,2,256,128]{5,4,3,2,1,0:T(8,128)(2,1)} custom-call(s32[4]{0:T(128)} %block_ref.1, s32[4]{0:T(128)} %limit_ref.1, s32[8]{0:T(128)} %flag_ref.1, bf16[2,256,768]{2,1,0:T(8,128)(2,1)} %bitcast.2, bf16[256,256]{1,0:T(8,128)(2,1)} %constant.6.clone.rows_hbm, bf16[256,256]{1,0:T(8,128)(2,1)} %constant.7.clone.cols_hbm), custom_call_target="tpu_custom_call" | custom-call | tf_op jit(solution)/shard_map/whiten_correlate/pallas_call | solution.py:331
  64.7 6.0 %lag_product.1 = bf16[4,256,1536]{2,1,0:T(8,128)(2,1)} custom-call(bf16[3,4,2,2,256,128]{5,4,3,2,1,0:T(8,128)(2,1)} %whiten_correlate.1.stack_hbm, bf16[2,768,768]{2,1,0:T(8,128)(2,1)} %constant.8.clone.table_hbm), custom_call_target="tpu_custom_call" | custom-call | tf_op jit(solution)/shard_map/lag_product/pallas_call | solution.py:386

commit v5 on v4

--- a/solution.py
+++ b/solution.py
@@ -48,18 +48,16 @@
 
 
 def whiten_into(spec_ref, flag_ref, rows_ref, cols_ref, out):
+    whole = []
+    for reim in range(2):
+        moved = jnp.dot(rows_ref[...], spec_ref[reim], preferred_element_type=jnp.float32).astype(jnp.bfloat16)
+        cut = [
+            jnp.dot(moved[:, 256 * b:256 * b + 256], cols_ref[...], preferred_element_type=jnp.float32)
+            for b in range(3)
+        ]
+        whole.append([jnp.concatenate([c[:, 128 * h:128 * h + 128] for c in cut], axis=1) for h in range(2)])
     for wp in range(4):
-        part = []
-        for reim in range(2):
-            moved = jnp.dot(rows_ref[pl.ds(wp * 64, 64), :], spec_ref[reim], preferred_element_type=jnp.float32)
-            moved = moved.astype(jnp.bfloat16)
-            cut = [
-                jnp.dot(moved[:, 256 * b:256 * b + 256], cols_ref[...], preferred_element_type=jnp.float32)
-                for b in range(3)
-            ]
-            even = jnp.concatenate([c[:, :128] for c in cut], axis=1)
-            odd = jnp.concatenate([c[:, 128:] for c in cut], axis=1)
-            part.append((even, odd))
+        part = [[v[64 * wp:64 * wp + 64] for v in pair] for pair in whole]
         (re0, re1), (im0, im1) = part
         p0 = re0 * re0 + im0 * im0
         p1 = re1 * re1 + im1 * im1
@@ -279,21 +277,20 @@
     exchange(1)
     m0 = choose(0)
     exchange(2)
+    m1 = choose(1)
     cross_over(1)
-    m1 = choose(1)
     f0 = gather(0, m0)
-    cross_over(2)
     relayed.append(relay(0))
     m2 = choose(2)
-    scatter(0, f0, (0, 1))
+    cross_over(2)
+    scatter(0, f0, range(R))
     f1 = gather(1, m1)
     f2 = gather(2, m2)
-    relayed.append(relay(1))
     receivers(0)
     arrived(0, 0)
-    scatter(0, (), (2, 3))
     compute(0, 0)
     scatter(1, f1, range(R))
+    relayed.append(relay(1))
     arrived(0, 1)
     compute(0, 1)
     scatter(2, f2, range(R))

time: 70.9 us -> 69.1 us (0.975)
  Pallas kernels: 70.7 us -> 68.9 us
    pallas_call x1, Pallas kernels: 64.7 us -> 62.9 us  [fused(): pl.pallas_call(kernel, out_shape=jax.ShapeDtypeStruct((3, R, 2, 2, 256, 1...]
where the time goes in v5:
time: 69.1 us; the launch traced here: 69 us
  Pallas kernels  68.9 us (100%)
    pallas_call x1, Pallas kernels, fused(): pl.pallas_call(kernel, out_shape=jax.ShapeDtypeStruct((3, R, 2, 2, 256, 1...  62.9 us
    pallas_call x1, Pallas kernels, lags(): pl.pallas_call(lag_kernel, out_shape=jax.ShapeDtypeStruct((R, 256, 2 * F)...  6.04 us

profile of v5, /device:TPU:0, one launch (start us, length us, event | category | flops | bytes accessed | tf_op | source)
XLA Modules:
  0.0 69.0 jit_solution(9423893619772107341)
XLA Ops:
  0.0 62.9 %whiten_correlate.1.stack_hbm = bf16[3,4,2,2,256,128]{5,4,3,2,1,0:T(8,128)(2,1)} custom-call(s32[4]{0:T(128)} %block_ref.1, s32[4]{0:T(128)} %limit_ref.1, s32[8]{0:T(128)} %flag_ref.1, bf16[2,256,768]{2,1,0:T(8,128)(2,1)} %bitcast.2, bf16[256,256]{1,0:T(8,128)(2,1)} %constant.6.clone.rows_hbm, bf16[256,256]{1,0:T(8,128)(2,1)} %constant.7.clone.cols_hbm), custom_call_target="tpu_custom_call" | custom-call | tf_op jit(solution)/shard_map/whiten_correlate/pallas_call | solution.py:328
  62.9 6.0 %lag_product.1 = bf16[4,256,1536]{2,1,0:T(8,128)(2,1)} custom-call(bf16[3,4,2,2,256,128]{5,4,3,2,1,0:T(8,128)(2,1)} %whiten_correlate.1.stack_hbm, bf16[2,768,768]{2,1,0:T(8,128)(2,1)} %constant.8.clone.table_hbm), custom_call_target="tpu_custom_call" | custom-call | tf_op jit(solution)/shard_map/lag_product/pallas_call | solution.py:383

commit v6 on v5

--- a/solution.py
+++ b/solution.py
@@ -278,29 +278,29 @@
     m0 = choose(0)
     exchange(2)
     m1 = choose(1)
+    f0 = gather(0, m0)
     cross_over(1)
-    f0 = gather(0, m0)
     relayed.append(relay(0))
     m2 = choose(2)
-    cross_over(2)
     scatter(0, f0, range(R))
     f1 = gather(1, m1)
     f2 = gather(2, m2)
+    cross_over(2)
     receivers(0)
     arrived(0, 0)
     compute(0, 0)
     scatter(1, f1, range(R))
-    relayed.append(relay(1))
     arrived(0, 1)
     compute(0, 1)
     scatter(2, f2, range(R))
-    relayed.append(relay(2))
+    relayed.append(relay(1))
 
     @pl.loop(2, R)
     def _(r):
         arrived(0, r)
         compute(0, r)
 
+    relayed.append(relay(2))
     for b in (1, 2):
         receivers(b)
 

time: 69.1 us -> 68.3 us (0.988)
  Pallas kernels: 68.9 us -> 68.2 us
    pallas_call x1, Pallas kernels: 62.9 us -> 62.2 us  [fused(): pl.pallas_call(kernel, out_shape=jax.ShapeDtypeStruct((3, R, 2, 2, 256, 1...]
where the time goes in v6:
time: 68.3 us; the launch traced here: 68.2 us
  Pallas kernels  68.2 us (100%)
    pallas_call x1, Pallas kernels, fused(): pl.pallas_call(kernel, out_shape=jax.ShapeDtypeStruct((3, R, 2, 2, 256, 1...  62.2 us
    pallas_call x1, Pallas kernels, lags(): pl.pallas_call(lag_kernel, out_shape=jax.ShapeDtypeStruct((R, 256, 2 * F)...  6.04 us

profile of v6, /device:TPU:0, one launch (start us, length us, event | category | flops | bytes accessed | tf_op | source)
XLA Modules:
  0.0 68.2 jit_solution(4448188501588892090)
XLA Ops:
  0.0 62.2 %whiten_correlate.1.stack_hbm = bf16[3,4,2,2,256,128]{5,4,3,2,1,0:T(8,128)(2,1)} custom-call(s32[4]{0:T(128)} %block_ref.1, s32[4]{0:T(128)} %limit_ref.1, s32[8]{0:T(128)} %flag_ref.1, bf16[2,256,768]{2,1,0:T(8,128)(2,1)} %bitcast.2, bf16[256,256]{1,0:T(8,128)(2,1)} %constant.6.clone.rows_hbm, bf16[256,256]{1,0:T(8,128)(2,1)} %constant.7.clone.cols_hbm), custom_call_target="tpu_custom_call" | custom-call | tf_op jit(solution)/shard_map/whiten_correlate/pallas_call | solution.py:328
  62.2 6.0 %lag_product.1 = bf16[4,256,1536]{2,1,0:T(8,128)(2,1)} custom-call(bf16[3,4,2,2,256,128]{5,4,3,2,1,0:T(8,128)(2,1)} %whiten_correlate.1.stack_hbm, bf16[2,768,768]{2,1,0:T(8,128)(2,1)} %constant.8.clone.table_hbm), custom_call_target="tpu_custom_call" | custom-call | tf_op jit(solution)/shard_map/lag_product/pallas_call | solution.py:383
